TPU v7x, 256 devices: a whole 4x4x8 slice. The times are simulated.
256 devices in a mesh: dp: 16 (over x, y_hi, core), tensor: 16 (over z, y_lo).
Axes of the slice: x: 4, y: 4 (y_hi: 2, y_lo: 2; y = y_hi * 2 + y_lo), z: 8, core: 2. Of those that a mesh axis runs over, the one named last changes fastest.
Arguments:
- tokens: bfloat16 [8192, 4096], P(('dp', 'tensor')), may hold values from -120 to 120
- norm_gain: float32 [4096], replicated, may hold values from 0.5 to 1.5
- w_gate: bfloat16 [4096, 8192], P('dp', 'tensor'), may hold values from -0.09375 to 0.09375
- w_up: bfloat16 [4096, 8192], P('dp', 'tensor'), may hold values from -0.09375 to 0.09375
- probes: bfloat16 [4096, 2, 8192], P('dp', None, 'tensor'), may hold values from -0.09375 to 0.09375
- cotangent: bfloat16 [8192, 8192], P('dp', 'tensor'), may hold values from -6 to 6
Outputs:
- hvp: float32 [4096, 2, 8192], P('dp', None, 'tensor')
All inputs are finite; a program needn't handle non-finite values.
Results may differ from a plain program's by a relative error of at most 0.014.
Values may be sent and summed in bfloat16 or wider, within the bound.
No kernel may reach another device: no remote copies, remote signals or barrier semaphores. Data moves between devices by JAX's collectives and lax.ppermute only.
A program may use at most 64 MiB of HBM per device.

v0:
```python
import math

import jax
import jax.numpy as jnp
from jax import lax
from jax.experimental import pallas as pl
from jax.experimental.pallas import tpu as pltpu
from jax.sharding import Mesh, PartitionSpec as P

NX, NYH, NC, NZ, NYL = 4, 2, 2, 8, 2
AXES = ("x", "yh", "c", "z", "yl")
VMEM_BYTES = 58 * 1024 * 1024


def ring_perm(spots, step):
    size = len(spots[0])
    return [
        (line[i], line[(i + sign * step) % size])
        for line, sign in zip(spots, (1, -1))
        for i in range(size)
    ]


def along_x(v, step):
    return lax.ppermute(
        v, ("x", "c"), ring_perm([[x * 2 + c for x in range(NX)] for c in range(NC)], step)
    )


def along_y(v, step):
    spots = [[(yh * 2 + c) * 2 + yl for yh in range(NYH) for yl in range(NYL)] for c in range(NC)]
    return lax.ppermute(v, ("yh", "c", "yl"), ring_perm(spots, step))


def swap_core(v):
    return lax.ppermute(v, "c", [(0, 1), (1, 0)])


def swap_yh(v):
    return lax.ppermute(v, "yh", [(0, 1), (1, 0)])


def norm_kernel(tokens, gain, out_a, out_b):
    x, c = lax.axis_index("x"), lax.axis_index("c")
    rows, depth = tokens.shape
    piece = depth // 16
    values = tokens[...].astype(jnp.float32)
    inverse = lax.rsqrt(jnp.mean(values * values, axis=1, keepdims=True) + 1e-05)
    for r in range(NX):
        xs = lax.rem(x + jnp.where(c == 0, NX - r, r), NX)
        for yh in range(NYH):
            for crel in range(NC):
                cs = jnp.where(crel == 0, c, 1 - c)
                source = pl.multiple_of((xs * 4 + yh * 2 + cs) * piece, piece)
                block = tokens[:, pl.ds(source, piece)].astype(jnp.float32)
                normed = (block * inverse * gain[:, pl.ds(source, piece)]).astype(jnp.bfloat16)
                b = r * 4 + crel * 2 + yh
                out_a[:, b * piece : (b + 1) * piece] = normed[: rows // 2]
                out_b[:, b * piece : (b + 1) * piece] = normed[rows // 2 :]


def normalize(tokens, gain):
    rows, depth = tokens.shape
    half = jax.ShapeDtypeStruct((rows // 2, depth), jnp.bfloat16)
    return pl.pallas_call(
        norm_kernel,
        out_shape=(half, half),
        in_specs=[
            pl.BlockSpec(memory_space=pltpu.VMEM),
            pl.BlockSpec(memory_space=pltpu.VMEM),
        ],
        out_specs=(pl.BlockSpec(memory_space=pltpu.VMEM),) * 2,
        compiler_params=pltpu.CompilerParams(vmem_limit_bytes=VMEM_BYTES),
        name="rms_norm",
    )(tokens, gain.reshape(1, depth))


def _a(dz):
    return [(i, dz, 0) for i in range(4)]


EARLY = (
    _a(0),
    _a(-1) + [(0, -2, 1)],
    _a(1) + [(0, 2, 1)],
    _a(-2) + [(0, -3, 1)],
    _a(2) + [(0, 3, 1)],
    _a(-3) + [(0, 4, 1)],
    _a(3),
    [(0, 0, 1)],
    [(0, -1, 1)],
    [(0, 1, 1)],
    [(2, 0, 1), (2, -1, 1), (2, 1, 1), (1, -2, 1), (1, 2, 1)],
    [(3, 0, 1), (3, -1, 1), (3, 1, 1), (2, -2, 1), (2, 2, 1), (1, -3, 1), (1, 3, 1)],
)
LATE = (
    [(1, 0, 1), (1, -1, 1), (1, 1, 1)],
    [(3, -2, 1), (3, 2, 1), (2, -3, 1), (2, 3, 1), (1, 4, 1)],
    [(3, -3, 1), (3, 3, 1), (3, 4, 1)],
    [(2, 4, 1)],
    _a(4),
)
BLOCK = 256


def rows_of(layout):
    return [16 * len(pieces) for pieces in layout]


def second_kernel(scale, layout, *refs):
    count = len(layout)
    arrays = refs[:count]
    keep, recv, cot_keep, cot_recv, out, nsc, wsc, cabs, csc, nsem, wsem, csem = refs[count:]
    x, yh, c, z, yl = (lax.axis_index(a) for a in AXES)
    y = yh * 2 + yl
    group, units = cot_keep.shape

    def copy(src, dst, sem):
        op = pltpu.make_async_copy(src, dst, sem)
        op.start()
        return op

    wait_c = [
        copy(cot_keep, cabs.at[pl.ds(pl.multiple_of(yh * group, group), group)], csem.at[0]),
        copy(cot_recv, cabs.at[pl.ds(pl.multiple_of((1 - yh) * group, group), group)], csem.at[1]),
    ]
    wait_w = []
    for xs in range(NX):
        r = lax.rem(jnp.where(c == 0, x - xs, xs - x) + NX, NX)
        for cs in range(NC):
            crel = jnp.where(c == cs, 0, 1)
            for mine, bunch in ((True, keep), (False, recv)):
                row = (r * 4 + crel * 2) * 256 + jnp.where(mine, yh, 1 - yh) * 256
                wait_w.append(
                    copy(
                        bunch.at[xs * 2 + cs],
                        wsc.at[pl.ds(pl.multiple_of(row, 256), 256)],
                        wsem.at[len(wait_w)],
                    )
                )
    wait_n, start = [], 0
    for i, (array, rows) in enumerate(zip(arrays, rows_of(layout))):
        op = copy(array.at[pl.ds(0, rows)], nsc.at[pl.ds(start, rows)], nsem.at[i])
        wait_n.append((start, op))
        start += rows
    for op in wait_c:
        op.wait()
    place = 0
    for pieces in layout:
        for dy, dz, half in pieces:
            ys = lax.rem(y + jnp.where(c == 0, 4 - dy, dy), 4)
            zs = lax.rem(z + dz + NZ, NZ)
            row = (ys // 2) * group + (zs * 2 + lax.rem(ys, 2)) * 32 + half * 16
            csc[place : place + 16, :] = cabs[pl.ds(pl.multiple_of(row, 16), 16), :]
            place += 16
    for op in wait_w:
        op.wait()
    for t in range(nsc.shape[0] // BLOCK):
        while wait_n and wait_n[0][0] < (t + 1) * BLOCK:
            wait_n.pop(0)[1].wait()
        block = nsc[t * BLOCK : (t + 1) * BLOCK, :]

        def mul(j):
            return jnp.dot(
                block, wsc[:, j * units : (j + 1) * units], preferred_element_type=jnp.float32
            )

        gate = mul(0)
        logistic = jax.nn.sigmoid(gate)
        curve = logistic * (1.0 - logistic) * (2.0 + gate * (1.0 - 2.0 * logistic))
        weighting = csc[t * BLOCK : (t + 1) * BLOCK, :].astype(jnp.float32) * curve * mul(1) * scale
        for p in range(2):
            second = weighting * mul(2 + p)
            out[p * units : (p + 1) * units, t * BLOCK : (t + 1) * BLOCK] = second.T.astype(
                jnp.bfloat16
            )


def second_factor(name, layout, arrays, keep, recv, cot_keep, cot_recv, scale):
    depth = arrays[0].shape[1]
    tokens = sum(rows_of(layout))
    group, units = cot_keep.shape
    operands = (*arrays, keep, recv, cot_keep, cot_recv)
    return pl.pallas_call(
        lambda *refs: second_kernel(scale, layout, *refs),
        out_shape=jax.ShapeDtypeStruct((2 * units, tokens), jnp.bfloat16),
        in_specs=[pl.BlockSpec(memory_space=pl.ANY)] * len(operands),
        out_specs=pl.BlockSpec(memory_space=pltpu.VMEM),
        scratch_shapes=[
            pltpu.VMEM((tokens, depth), jnp.bfloat16),
            pltpu.VMEM((depth, 4 * units), jnp.bfloat16),
            pltpu.VMEM((2 * group, units), jnp.bfloat16),
            pltpu.VMEM((tokens, units), jnp.bfloat16),
            pltpu.SemaphoreType.DMA((len(layout),)),
            pltpu.SemaphoreType.DMA((16,)),
            pltpu.SemaphoreType.DMA((2,)),
        ],
        compiler_params=pltpu.CompilerParams(vmem_limit_bytes=32 * 1024 * 1024),
        cost_estimate=pl.CostEstimate(
            flops=2**20, bytes_accessed=2**20, transcendentals=0
        ),
        name=name,
    )(*operands)


def partial_kernel(early_count, *refs):
    arrays, second_e, second_l, own, sib = refs[:-4], refs[-4], refs[-3], refs[-2], refs[-1]
    early = jnp.concatenate([a[...] for a in arrays[:early_count]], axis=0)
    late = jnp.concatenate([a[...] for a in arrays[early_count:]], axis=0)
    result = jnp.dot(second_e[...], early, preferred_element_type=jnp.float32)
    result = result + jnp.dot(second_l[...], late, preferred_element_type=jnp.float32)
    result = result.astype(jnp.bfloat16)
    step = pl.program_id(0)

    @pl.when(step == 0)
    def _():
        own[...] = result

    @pl.when(step == 1)
    def _():
        sib[...] = result


def partials(arrays, second_e, second_l, r):
    width = second_e.shape[0]
    rows = rows_of(EARLY + LATE)
    half = jax.ShapeDtypeStruct((width, 512), jnp.bfloat16)
    whole = pl.BlockSpec((width, 512), lambda j: (0, 0))
    return pl.pallas_call(
        lambda *refs: partial_kernel(len(EARLY), *refs),
        grid=(2,),
        out_shape=(half, half),
        in_specs=[pl.BlockSpec((n, 512), lambda j: (0, r * 2 + j)) for n in rows]
        + [pl.BlockSpec(a.shape, lambda j: (0, 0)) for a in (second_e, second_l)],
        out_specs=(whole, whole),
        compiler_params=pltpu.CompilerParams(vmem_limit_bytes=24 * 1024 * 1024),
        cost_estimate=pl.CostEstimate(
            flops=2**20, bytes_accessed=2**20, transcendentals=0
        ),
        name="partials_%d" % r,
    )(*arrays, second_e, second_l)


def final_kernel(m0, m1, m2, m3, got, out):
    units = out.shape[2] // 2
    yh = lax.axis_index("yh")
    mine = m0[...]
    for m in (m1, m2, m3):
        mine = mine + m[...].astype(jnp.float32)
    got = got[...].astype(jnp.float32)
    low, high = jnp.where(yh == 0, mine, got), jnp.where(yh == 0, got, mine)
    for p in range(2):
        rows = slice(p * units, (p + 1) * units)
        out[:, p, 0:units] = low[rows].T
        out[:, p, units : 2 * units] = high[rows].T


def finish(mine, got):
    width, rows = got.shape
    vmem = pl.BlockSpec(memory_space=pltpu.VMEM)
    return pl.pallas_call(
        final_kernel,
        out_shape=jax.ShapeDtypeStruct((rows, 2, width), jnp.float32),
        in_specs=[vmem] * 5,
        out_specs=vmem,
        compiler_params=pltpu.CompilerParams(vmem_limit_bytes=24 * 1024 * 1024),
        name="finish",
    )(*mine, got)


def lay_kernel(parts, *refs):
    outs = refs[len(refs) - len(parts) :]
    for part, out in zip(parts, outs):
        start = 0
        for i in part:
            n = refs[i].shape[0]
            out[start : start + n, :] = refs[i][...]
            start += n


def lay(name, pieces, parts):
    depth = pieces[0][0].shape[1]
    vmem = pl.BlockSpec(memory_space=pltpu.VMEM)
    return pl.pallas_call(
        lambda *refs: lay_kernel(parts, *refs),
        grid=(1,),
        out_shape=[
            jax.ShapeDtypeStruct((sum(pieces[i][2] for i in part), depth), jnp.bfloat16)
            for part in parts
        ],
        in_specs=[
            pl.BlockSpec((n, depth), lambda j, at=first // n: (at, 0)) for _, first, n in pieces
        ],
        out_specs=[
            pl.BlockSpec((sum(pieces[i][2] for i in part), depth), lambda j: (0, 0))
            for part in parts
        ],
        compiler_params=pltpu.CompilerParams(vmem_limit_bytes=24 * 1024 * 1024),
        name=name,
    )(*[a for a, _, _ in pieces])


def shift_z(v, step):
    return lax.ppermute(v, "z", [(i, (i + step) % NZ) for i in range(NZ)])


def per_device(tokens, norm_gain, w_gate, w_up, probes, cotangent):
    yh, c = lax.axis_index("yh"), lax.axis_index("c")
    units = w_gate.shape[1] // 2
    ordered = lax.optimization_barrier

    def half_of(which):
        return jnp.concatenate(
            [lax.dynamic_slice_in_dim(a, which * units, units, 1) for a in (w_gate, w_up, p0, p1)],
            axis=1,
        )

    a0, b0 = normalize(tokens, norm_gain)
    a0, b0, w_gate, w_up, probes, cotangent = ordered(
        (a0, b0, w_gate, w_up, probes, cotangent)
    )
    p0, p1 = probes[:, 0, :], probes[:, 1, :]
    w_keep, w_send = half_of(yh), half_of(1 - yh)
    cot_keep = lax.dynamic_slice_in_dim(cotangent, yh * units, units, 1)
    cot_send = lax.dynamic_slice_in_dim(cotangent, (1 - yh) * units, units, 1)
    keep = lax.all_gather(w_keep, ("x", "c"))

    ya = [along_y(a0, i) for i in (1, 2, 3)]
    bm, bp = shift_z(b0, 1), shift_z(b0, -1)
    *ya, bm, bp, w_send, b0 = ordered((*ya, bm, bp, w_send, b0))

    w_recv = swap_yh(w_send)
    up0, down0, y0 = lay(
        "lay_1",
        [(v, 0, 16) for v in (a0, *ya, bm, bp, b0)],
        ((0, 1, 2, 3, 4), (0, 1, 2, 3, 5), (6, 4, 5)),
    )
    up1, down1 = shift_z(up0, 1), shift_z(down0, -1)
    y1 = along_y(y0, 1)
    up1, down1, y1, w_recv = ordered((up1, down1, y1, w_recv))
    recv = lax.all_gather(w_recv, ("x", "c"))

    up2, down2 = shift_z(up1, 1), shift_z(down1, -1)
    (y,) = lay("lay_2", [(y1, 0, 48), (up1, 64, 16), (down1, 64, 16)], ((0, 1, 2),))
    y2 = along_y(y, 1)
    up2, down2, y2, cot_send = ordered((up2, down2, y2, cot_send))
    cot_recv = swap_yh(cot_send)

    up3, down3 = shift_z(up2, 1), shift_z(down2, -1)
    (y,) = lay("lay_3", [(y2, 0, 80), (up2, 64, 16), (down2, 64, 16)], ((0, 1, 2),))
    y3 = along_y(y, 1)
    up3, down3, y3, cot_recv, keep, recv = ordered((up3, down3, y3, cot_recv, keep, recv))

    a4 = lax.ppermute(
        jnp.where(c == 0, up3[:64], down3[:64]),
        ("c", "z"),
        ring_perm([[i * NZ + z for z in range(NZ)] for i in range(NC)], 1),
    )
    y, around, across = lay(
        "lay_4",
        [(y3, 48, 16), (y3, 64, 16), (y3, 80, 16), (y3, 96, 16)]
        + [(up3, 64, 16), (up2, 64, 16), (down2, 64, 16)],
        ((0, 1, 2, 3, 4), (5, 6, 4), (4,)),
    )
    y4, y5, y6 = along_y(y, 1), along_y(around, 3), along_y(across, 2)
    early = (up0, up1, down1, up2, down2, up3, down3, b0, bm, bp, y2, y3)
    late = (y1, y4, y5, y6, a4)

    scale = 1.0 / math.sqrt(cotangent.shape[0] * NX * NYH * NC)
    rest = (keep, recv, cot_keep, cot_recv, scale)
    second_e = second_factor("second_early", EARLY, early, *rest)
    second_l = second_factor("second_late", LATE, late, *rest)
    own, sib, first, last = {}, {}, {}, {}
    arrays = early + late

    def add_cores(r):
        other = swap_core(sib[(NX - r) % NX])
        both = own[r].astype(jnp.float32) + other.astype(jnp.float32)
        pair = [lax.dynamic_slice_in_dim(both, w * 256, 256, 1) for w in (1 - yh, yh)]
        if r:
            pair = [v.astype(jnp.bfloat16) for v in pair]
        return ordered(pair[0]), ordered(pair[1])

    own[2], sib[2] = partials(arrays, second_e, second_l, 2)
    own[3], sib[3] = partials(arrays, second_e, second_l, 3)
    first[2], last[2] = add_cores(2)
    first[2], last[2], second_l = ordered((first[2], last[2], second_l))
    own[1], sib[1] = partials(arrays, second_e, second_l, 1)
    first[1], last[1] = add_cores(1)
    first[1], second_l = ordered((first[1], second_l))
    own[0], sib[0] = partials(arrays, second_e, second_l, 0)
    first[3], last[3] = add_cores(3)
    first[0], last[0] = add_cores(0)
    last[2] = along_x(last[2], NX - 2)
    for r in (2, 1, 3):
        first[r] = along_x(first[r], NX - r)
    *arrived, last[1], last[3] = ordered((*(first[r] for r in range(NX)), last[1], last[3]))
    total = sum(v.astype(jnp.float32) for v in arrived)
    for r in (1, 3):
        last[r] = along_x(last[r], NX - r)
    got = swap_yh(total.astype(jnp.bfloat16))
    return finish([last[r] for r in range(NX)], got)


def solution(mesh):
    inner = Mesh(mesh.devices.reshape(NX, NYH, NC, NZ, NYL), AXES)
    dp, tensor = ("x", "yh", "c"), ("z", "yl")
    in_specs = (
        P(dp + tensor, None),
        P(),
        P(dp, tensor),
        P(dp, tensor),
        P(dp, None, tensor),
        P(dp, tensor),
    )
    return jax.shard_map(
        per_device, mesh=inner, in_specs=in_specs, out_specs=P(dp, None, tensor), check_vma=False
    )
```

profile of v0, /device:TPU:2, one launch (start us, length us, event | category | flops | bytes accessed | tf_op | source)
XLA Modules:
  0.0 165.6 jit_solution(4436512398425412156)
XLA Ops:
  13.4 2.9 %collective-permute-start.1 = (bf16[16,4096]{1,0:T(8,128)(2,1)S(1)}, bf16[16,4096]{1,0:T(8,128)(2,1)S(1)}, u32[]{:S(2)}, u32[]{:S(2)}) collective-permute-start(bf16[16,4096]{1,0:T(8,128)(2,1)S(1)} %copy-done.17), channel_id=1, source_target_pairs={{0,32},{1,33},{32,0},{33,1},{16,48},{17,49},{48,16},{49,17},{2,34}... | collective-permute-start | bytes 393224 | tf_op jit(solution)/shard_map/ppermute | solution.py:32
  19.5 3.9 %collective-permute-start.4 = (bf16[16,4096]{1,0:T(8,128)(2,1)S(1)}, bf16[16,4096]{1,0:T(8,128)(2,1)S(1)}, u32[]{:S(2)}, u32[]{:S(2)}) collective-permute-start(bf16[16,4096]{1,0:T(8,128)(2,1)S(1)} %copy-done.10), channel_id=1, source_target_pairs={{0,14},{2,0},{4,2},{6,4},{8,6},{10,8},{12,10},{14,12},{1,15},{3,1}... | collective-permute-start | bytes 393224 | tf_op jit(solution)/shard_map/ppermute | solution.py:304
  23.6 2.8 %collective-permute-done.3.refs_4_.refs_8_ = bf16[16,4096]{1,0:T(8,128)(2,1)S(1)} collective-permute-done((bf16[16,4096]{1,0:T(8,128)(2,1)S(1)}, bf16[16,4096]{1,0:T(8,128)(2,1)S(1)}, u32[]{:S(2)}, u32[]{:S(2)}) %collective-permute-start.3) | collective-permute-done | bytes 131104 | tf_op jit(solution)/shard_map/ppermute | solution.py:304
  26.6 3.3 %collective-permute-start.6 = (bf16[80,4096]{1,0:T(8,128)(2,1)S(1)}, bf16[80,4096]{1,0:T(8,128)(2,1)S(1)}, u32[]{:S(2)}, u32[]{:S(2)}) collective-permute-start(bf16[80,4096]{1,0:T(8,128)(2,1)S(1)} %get-tuple-element.73), channel_id=1, source_target_pairs={{0,14},{2,0},{4,2},{6,4},{8,6},{10,8},{12,10},{14,12},{1,15},{3,1}... | collective-permute-start | bytes 1966088 | tf_op jit(solution)/shard_map/ppermute | solution.py:304
  31.5 16.5 %collective-permute-done.7.refs_0_.refs_12_ = bf16[48,4096]{1,0:T(8,128)(2,1)S(1)} collective-permute-done((bf16[48,4096]{1,0:T(8,128)(2,1)S(1)}, bf16[48,4096]{1,0:T(8,128)(2,1)S(1)}, u32[]{:S(2)}, u32[]{:S(2)}) %collective-permute-start.7) | collective-permute-done | bytes 393248 | tf_op jit(solution)/shard_map/ppermute | solution.py:32
  52.9 7.7 %collective-permute-done.11.refs_0_.refs_10_ = bf16[80,4096]{1,0:T(8,128)(2,1)S(1)} collective-permute-done((bf16[80,4096]{1,0:T(8,128)(2,1)S(1)}, bf16[80,4096]{1,0:T(8,128)(2,1)S(1)}, u32[]{:S(2)}, u32[]{:S(2)}) %collective-permute-start.11) | collective-permute-done | bytes 655392 | tf_op jit(solution)/shard_map/ppermute | solution.py:32
  60.6 5.9 %collective-permute-done.10.refs_2_.refs_6_.refs_4_ = bf16[80,4096]{1,0:T(8,128)(2,1)S(1)} collective-permute-done((bf16[80,4096]{1,0:T(8,128)(2,1)S(1)}, bf16[80,4096]{1,0:T(8,128)(2,1)S(1)}, u32[]{:S(2)}, u32[]{:S(2)}) %collective-permute-start.10) | collective-permute-done | bytes 655392 | tf_op jit(solution)/shard_map/ppermute | solution.py:304
  66.5 2.6 %collective-permute-done.9.refs_1_.refs_5_.refs_3_ = bf16[80,4096]{1,0:T(8,128)(2,1)S(1)} collective-permute-done((bf16[80,4096]{1,0:T(8,128)(2,1)S(1)}, bf16[80,4096]{1,0:T(8,128)(2,1)S(1)}, u32[]{:S(2)}, u32[]{:S(2)}) %collective-permute-start.9) | collective-permute-done | bytes 655392 | tf_op jit(solution)/shard_map/ppermute | solution.py:304
  70.2 3.2 %collective-permute-start.13 = (bf16[80,4096]{1,0:T(8,128)(2,1)S(1)}, bf16[80,4096]{1,0:T(8,128)(2,1)}, u32[]{:S(2)}, u32[]{:S(2)}) collective-permute-start(bf16[80,4096]{1,0:T(8,128)(2,1)S(1)} %collective-permute-done.10.refs_2_.refs_6_.refs_4_), channel_id=1, source_target_pairs={{0,14},{2,0},{4,2},{6,4},{8,6},{10,8},{12,10},{14,12},{1,15},{3,1}... | collective-permute-start | bytes 1966088 | tf_op jit(solution)/shard_map/ppermute | solution.py:304
  75.1 14.2 %collective-permute-done.15.refs_15_.refs_8_ = bf16[512,256]{1,0:T(8,128)(2,1)} collective-permute-done((bf16[512,256]{1,0:T(8,128)(2,1)}, bf16[512,256]{1,0:T(8,128)(2,1)}, u32[]{:S(2)}, u32[]{:S(2)}) %collective-permute-start.15) | collective-permute-done | bytes 262176 | tf_op jit(solution)/shard_map/ppermute | solution.py:40
  92.1 3.1 %collective-permute-start.17 = (bf16[48,4096]{1,0:T(8,128)(2,1)S(1)}, bf16[48,4096]{1,0:T(8,128)(2,1)S(1)}, u32[]{:S(2)}, u32[]{:S(2)}) collective-permute-start(bf16[48,4096]{1,0:T(8,128)(2,1)S(1)} %get-tuple-element.89), channel_id=1, source_target_pairs={{0,33},{1,0},{32,1},{33,32},{16,17},{17,48},{48,49},{49,16},{2,35}... | collective-permute-start | bytes 1179656 | tf_op jit(solution)/shard_map/ppermute | solution.py:32
  95.4 2.2 %copy-done.5 = bf16[2048,1024]{1,0:T(8,128)(2,1)S(1)} copy-done((bf16[2048,1024]{1,0:T(8,128)(2,1)S(1)}, bf16[2048,1024]{1,0:T(8,128)(2,1)}, u32[]{:S(2)}) %copy-start.5) | copy-done | bytes 4194328
  97.6 10.7 %second_early.1.refs_17_ = bf16[512,768]{1,0:T(8,128)(2,1)S(1)} custom-call(bf16[80,4096]{1,0:T(8,128)(2,1)S(1)} %copy-done.7, bf16[80,4096]{1,0:T(8,128)(2,1)S(1)} %collective-permute-done.5.refs_1_, bf16[80,4096]{1,0:T(8,128)(2,1)S(1)} %copy-done.1, bf16[80,4096]{1,0:T(8,128)(2,1)S(1)} %collective-permute-done.9.refs_1_.refs_5_.refs_3_, ...), custom_call_target="tpu_custom_call" | custom-call | flops 1048576 | bytes 1048576 | tf_op jit(solution)/shard_map/second_early/pallas_call | solution.py:184
  109.6 4.2 %second_late.1.refs_18_ = bf16[512,256]{1,0:T(8,128)(2,1)S(1)} custom-call(bf16[48,4096]{1,0:T(8,128)(2,1)S(1)} %copy-done.9, bf16[80,4096]{1,0:T(8,128)(2,1)S(1)} %collective-permute-done.16.refs_1_.refs_13_, bf16[48,4096]{1,0:T(8,128)(2,1)S(1)} %collective-permute-done.17.refs_2_.refs_14_, bf16[16,4096]{1,0:T(8,128)(2,1)S(1)} %collective-permute-done.18.refs_3_.refs_15_, ...), custom_call_target="tpu_custom_call" | custom-call | flops 1048576 | bytes 1048576 | tf_op jit(solution)/shard_map/second_late/pallas_call | solution.py:184
  113.8 2.5 %partials_2.1 = (bf16[512,512]{1,0:T(8,128)(2,1)S(1)}, bf16[512,512]{1,0:T(8,128)(2,1)S(1)}) custom-call(bf16[80,4096]{1,0:T(8,128)(2,1)S(1)} %copy-done.7, bf16[80,4096]{1,0:T(8,128)(2,1)S(1)} %collective-permute-done.5.refs_1_, bf16[80,4096]{1,0:T(8,128)(2,1)S(1)} %copy-done.1, bf16[80,4096]{1,0:T(8,128)(2,1)S(1)} %collective-permute-done.9.refs_1_.refs_5_.refs_3_, ...), custom_call_target="tpu_custom_call" | custom-call | flops 1048576 | bytes 1048576 | tf_op jit(solution)/shard_map/partials_2/pallas_call | solution.py:229
  116.4 2.5 %partials_3.1 = (bf16[512,512]{1,0:T(8,128)(2,1)S(1)}, bf16[512,512]{1,0:T(8,128)(2,1)S(1)}) custom-call(bf16[80,4096]{1,0:T(8,128)(2,1)S(1)} %copy-done.7, bf16[80,4096]{1,0:T(8,128)(2,1)S(1)} %collective-permute-done.5.refs_1_, bf16[80,4096]{1,0:T(8,128)(2,1)S(1)} %copy-done.1, bf16[80,4096]{1,0:T(8,128)(2,1)S(1)} %collective-permute-done.9.refs_1_.refs_5_.refs_3_, ...), custom_call_target="tpu_custom_call" | custom-call | flops 1048576 | bytes 1048576 | tf_op jit(solution)/shard_map/partials_3/pallas_call | solution.py:229
  119.9 2.5 %partials_1.1 = (bf16[512,512]{1,0:T(8,128)(2,1)S(1)}, bf16[512,512]{1,0:T(8,128)(2,1)S(1)}) custom-call(bf16[80,4096]{1,0:T(8,128)(2,1)S(1)} %copy-done.7, bf16[80,4096]{1,0:T(8,128)(2,1)S(1)} %collective-permute-done.5.refs_1_, bf16[80,4096]{1,0:T(8,128)(2,1)S(1)} %copy-done.1, bf16[80,4096]{1,0:T(8,128)(2,1)S(1)} %collective-permute-done.9.refs_1_.refs_5_.refs_3_, ...), custom_call_target="tpu_custom_call" | custom-call | flops 1048576 | bytes 1048576 | tf_op jit(solution)/shard_map/partials_1/pallas_call | solution.py:229
  122.8 2.5 %partials_0.1 = (bf16[512,512]{1,0:T(8,128)(2,1)S(1)}, bf16[512,512]{1,0:T(8,128)(2,1)S(1)}) custom-call(bf16[80,4096]{1,0:T(8,128)(2,1)S(1)} %copy-done.7, bf16[80,4096]{1,0:T(8,128)(2,1)S(1)} %collective-permute-done.5.refs_1_, bf16[80,4096]{1,0:T(8,128)(2,1)S(1)} %copy-done.1, bf16[80,4096]{1,0:T(8,128)(2,1)S(1)} %collective-permute-done.9.refs_1_.refs_5_.refs_3_, ...), custom_call_target="tpu_custom_call" | custom-call | flops 1048576 | bytes 1048576 | tf_op jit(solution)/shard_map/partials_0/pallas_call | solution.py:229
  126.7 2.1 %collective-permute-start.24 = (bf16[512,256]{1,0:T(8,128)(2,1)S(1)}, bf16[512,256]{1,0:T(8,128)(2,1)S(1)}, u32[]{:S(2)}, u32[]{:S(2)}) collective-permute-start(bf16[512,256]{1,0:T(8,128)(2,1)S(1)} %get-tuple-element.103), channel_id=1, source_target_pairs={{0,128},{64,192},{128,0},{192,64},{16,144},{80,208},{144,16},{208,... | collective-permute-start | bytes 786440 | tf_op jit(solution)/shard_map/ppermute | solution.py:25
  133.2 7.5 %collective-permute-done.24 = bf16[512,256]{1,0:T(8,128)(2,1)S(1)} collective-permute-done((bf16[512,256]{1,0:T(8,128)(2,1)S(1)}, bf16[512,256]{1,0:T(8,128)(2,1)S(1)}, u32[]{:S(2)}, u32[]{:S(2)}) %collective-permute-start.24) | collective-permute-done | bytes 262176 | tf_op jit(solution)/shard_map/ppermute | solution.py:25
  140.6 4.7 %collective-permute-done.26 = bf16[512,256]{1,0:T(8,128)(2,1)S(1)} collective-permute-done((bf16[512,256]{1,0:T(8,128)(2,1)S(1)}, bf16[512,256]{1,0:T(8,128)(2,1)S(1)}, u32[]{:S(2)}, u32[]{:S(2)}) %collective-permute-start.26) | collective-permute-done | bytes 262176 | tf_op jit(solution)/shard_map/ppermute | solution.py:25
  145.5 2.3 %collective-permute-start.30 = (bf16[512,256]{1,0:T(8,128)(2,1)S(1)}, bf16[512,256]{1,0:T(8,128)(2,1)S(1)}, u32[]{:S(2)}, u32[]{:S(2)}) collective-permute-start(bf16[512,256]{1,0:T(8,128)(2,1)S(1)} %add_convert_fusion), channel_id=1, source_target_pairs={{0,32},{32,0},{1,33},{33,1},{2,34},{34,2},{3,35},{35,3},{4,36},{36... | collective-permute-start | bytes 786440 | tf_op jit(solution)/shard_map/ppermute | solution.py:40
  147.9 3.0 %collective-permute-start.27 = (bf16[512,256]{1,0:T(8,128)(2,1)S(1)}, bf16[512,256]{1,0:T(8,128)(2,1)S(1)}, u32[]{:S(2)}, u32[]{:S(2)}) collective-permute-start(bf16[512,256]{1,0:T(8,128)(2,1)S(1)} %get-tuple-element.106), channel_id=1, source_target_pairs={{0,192},{64,0},{128,64},{192,128},{16,80},{80,144},{144,208},{208,... | collective-permute-start | bytes 786440 | tf_op jit(solution)/shard_map/ppermute | solution.py:25
  150.9 5.3 %collective-permute-done.30.got = bf16[512,256]{1,0:T(8,128)(2,1)S(1)} collective-permute-done((bf16[512,256]{1,0:T(8,128)(2,1)S(1)}, bf16[512,256]{1,0:T(8,128)(2,1)S(1)}, u32[]{:S(2)}, u32[]{:S(2)}) %collective-permute-start.30) | collective-permute-done | bytes 262176 | tf_op jit(solution)/shard_map/ppermute | solution.py:40
  (109 shorter events, 33.4 us)
Async XLA Ops:
  6.5 84.0 %all-gather.5.cloned.1.call-start = ((), (), s32[]{:S(2)}) async-start(), calls=%async_computation | async-start | bytes 4718592 | tf_op jit(solution)/shard_map/all_gather | solution.py:326
  11.6 78.9 %all-gather.7.cloned.1.call-start = ((), (), s32[]{:S(2)}) async-start(), calls=%async_computation.1 | async-start | bytes 4718592 | tf_op jit(solution)/shard_map/all_gather | solution.py:341
  11.7 11.8 %collective-permute-start = (bf16[16,4096]{1,0:T(8,128)(2,1)S(1)}, bf16[16,4096]{1,0:T(8,128)(2,1)S(1)}, u32[]{:S(2)}, u32[]{:S(2)}) collective-permute-start(bf16[16,4096]{1,0:T(8,128)(2,1)S(1)} %copy-done.17), channel_id=1, source_target_pairs={{0,1},{1,32},{32,33},{33,0},{16,49},{17,16},{48,17},{49,48},{2,3},... | collective-permute-start | bytes 393224 | tf_op jit(solution)/shard_map/ppermute | solution.py:32
  13.4 10.2 %collective-permute-start.1 = (bf16[16,4096]{1,0:T(8,128)(2,1)S(1)}, bf16[16,4096]{1,0:T(8,128)(2,1)S(1)}, u32[]{:S(2)}, u32[]{:S(2)}) collective-permute-start(bf16[16,4096]{1,0:T(8,128)(2,1)S(1)} %copy-done.17), channel_id=1, source_target_pairs={{0,32},{1,33},{32,0},{33,1},{16,48},{17,49},{48,16},{49,17},{2,34}... | collective-permute-start | bytes 393224 | tf_op jit(solution)/shard_map/ppermute | solution.py:32
  17.6 8.8 %collective-permute-start.3 = (bf16[16,4096]{1,0:T(8,128)(2,1)S(1)}, bf16[16,4096]{1,0:T(8,128)(2,1)S(1)}, u32[]{:S(2)}, u32[]{:S(2)}) collective-permute-start(bf16[16,4096]{1,0:T(8,128)(2,1)S(1)} %copy-done.10), channel_id=1, source_target_pairs={{0,2},{2,4},{4,6},{6,8},{8,10},{10,12},{12,14},{14,0},{1,3},{3,5},... | collective-permute-start | bytes 393224 | tf_op jit(solution)/shard_map/ppermute | solution.py:304
  26.5 21.5 %collective-permute-start.5 = (bf16[80,4096]{1,0:T(8,128)(2,1)S(1)}, bf16[80,4096]{1,0:T(8,128)(2,1)S(1)}, u32[]{:S(2)}, u32[]{:S(2)}) collective-permute-start(bf16[80,4096]{1,0:T(8,128)(2,1)S(1)} %get-tuple-element.72.refs_0_), channel_id=1, source_target_pairs={{0,2},{2,4},{4,6},{6,8},{8,10},{10,12},{12,14},{14,0},{1,3},{3,5},... | collective-permute-start | bytes 1966088 | tf_op jit(solution)/shard_map/ppermute | solution.py:304
  26.6 21.4 %collective-permute-start.6 = (bf16[80,4096]{1,0:T(8,128)(2,1)S(1)}, bf16[80,4096]{1,0:T(8,128)(2,1)S(1)}, u32[]{:S(2)}, u32[]{:S(2)}) collective-permute-start(bf16[80,4096]{1,0:T(8,128)(2,1)S(1)} %get-tuple-element.73), channel_id=1, source_target_pairs={{0,14},{2,0},{4,2},{6,4},{8,6},{10,8},{12,10},{14,12},{1,15},{3,1}... | collective-permute-start | bytes 1966088 | tf_op jit(solution)/shard_map/ppermute | solution.py:304
  29.9 18.1 %collective-permute-start.8 = (bf16[256,1024]{1,0:T(8,128)(2,1)S(1)}, bf16[256,1024]{1,0:T(8,128)(2,1)}, u32[]{:S(2)}, u32[]{:S(2)}) collective-permute-start(bf16[256,1024]{1,0:T(8,128)(2,1)S(1)} %pad_maximum_fusion), channel_id=1, source_target_pairs={{0,32},{32,0},{1,33},{33,1},{2,34},{34,2},{3,35},{35,3},{4,36},{36... | collective-permute-start | bytes 1572872 | tf_op jit(solution)/shard_map/ppermute | solution.py:40
  30.6 17.4 %collective-permute-start.7 = (bf16[48,4096]{1,0:T(8,128)(2,1)S(1)}, bf16[48,4096]{1,0:T(8,128)(2,1)S(1)}, u32[]{:S(2)}, u32[]{:S(2)}) collective-permute-start(bf16[48,4096]{1,0:T(8,128)(2,1)S(1)} %get-tuple-element.74), channel_id=1, source_target_pairs={{0,1},{1,32},{32,33},{33,0},{16,49},{17,16},{48,17},{49,48},{2,3},... | collective-permute-start | bytes 1179656 | tf_op jit(solution)/shard_map/ppermute | solution.py:32
  48.8 11.8 %collective-permute-start.11 = (bf16[80,4096]{1,0:T(8,128)(2,1)S(1)}, bf16[80,4096]{1,0:T(8,128)(2,1)S(1)}, u32[]{:S(2)}, u32[]{:S(2)}) collective-permute-start(bf16[80,4096]{1,0:T(8,128)(2,1)S(1)} %lay_2.1), channel_id=1, source_target_pairs={{0,1},{1,32},{32,33},{33,0},{16,49},{17,16},{48,17},{49,48},{2,3},... | collective-permute-start | bytes 1966088 | tf_op jit(solution)/shard_map/ppermute | solution.py:32
  49.0 17.5 %collective-permute-start.10 = (bf16[80,4096]{1,0:T(8,128)(2,1)S(1)}, bf16[80,4096]{1,0:T(8,128)(2,1)S(1)}, u32[]{:S(2)}, u32[]{:S(2)}) collective-permute-start(bf16[80,4096]{1,0:T(8,128)(2,1)S(1)} %collective-permute-done.6.refs_2_), channel_id=1, source_target_pairs={{0,14},{2,0},{4,2},{6,4},{8,6},{10,8},{12,10},{14,12},{1,15},{3,1}... | collective-permute-start | bytes 1966088 | tf_op jit(solution)/shard_map/ppermute | solution.py:304
  50.7 18.4 %collective-permute-start.9 = (bf16[80,4096]{1,0:T(8,128)(2,1)S(1)}, bf16[80,4096]{1,0:T(8,128)(2,1)S(1)}, u32[]{:S(2)}, u32[]{:S(2)}) collective-permute-start(bf16[80,4096]{1,0:T(8,128)(2,1)S(1)} %collective-permute-done.5.refs_1_), channel_id=1, source_target_pairs={{0,2},{2,4},{4,6},{6,8},{8,10},{10,12},{12,14},{14,0},{1,3},{3,5},... | collective-permute-start | bytes 1966088 | tf_op jit(solution)/shard_map/ppermute | solution.py:304
  70.1 20.4 %collective-permute-start.14 = (bf16[112,4096]{1,0:T(8,128)(2,1)}, bf16[112,4096]{1,0:T(8,128)(2,1)S(1)}, u32[]{:S(2)}, u32[]{:S(2)}) collective-permute-start(bf16[112,4096]{1,0:T(8,128)(2,1)} %lay_3.1), channel_id=1, source_target_pairs={{0,1},{1,32},{32,33},{33,0},{16,49},{17,16},{48,17},{49,48},{2,3},... | collective-permute-start | bytes 2752520 | tf_op jit(solution)/shard_map/ppermute | solution.py:32
  70.1 19.2 %collective-permute-start.12 = (bf16[80,4096]{1,0:T(8,128)(2,1)S(1)}, bf16[80,4096]{1,0:T(8,128)(2,1)S(1)}, u32[]{:S(2)}, u32[]{:S(2)}) collective-permute-start(bf16[80,4096]{1,0:T(8,128)(2,1)S(1)} %collective-permute-done.9.refs_1_.refs_5_.refs_3_), channel_id=1, source_target_pairs={{0,2},{2,4},{4,6},{6,8},{8,10},{10,12},{12,14},{14,0},{1,3},{3,5},... | collective-permute-start | bytes 1966088 | tf_op jit(solution)/shard_map/ppermute | solution.py:304
  70.2 19.1 %collective-permute-start.13 = (bf16[80,4096]{1,0:T(8,128)(2,1)S(1)}, bf16[80,4096]{1,0:T(8,128)(2,1)}, u32[]{:S(2)}, u32[]{:S(2)}) collective-permute-start(bf16[80,4096]{1,0:T(8,128)(2,1)S(1)} %collective-permute-done.10.refs_2_.refs_6_.refs_4_), channel_id=1, source_target_pairs={{0,14},{2,0},{4,2},{6,4},{8,6},{10,8},{12,10},{14,12},{1,15},{3,1}... | collective-permute-start | bytes 1966088 | tf_op jit(solution)/shard_map/ppermute | solution.py:304
  73.4 15.8 %collective-permute-start.15 = (bf16[512,256]{1,0:T(8,128)(2,1)}, bf16[512,256]{1,0:T(8,128)(2,1)}, u32[]{:S(2)}, u32[]{:S(2)}) collective-permute-start(bf16[512,256]{1,0:T(8,128)(2,1)} %get-tuple-element.83), channel_id=1, source_target_pairs={{0,32},{32,0},{1,33},{33,1},{2,34},{34,2},{3,35},{35,3},{4,36},{36... | collective-permute-start | bytes 786440 | tf_op jit(solution)/shard_map/ppermute | solution.py:40
  90.7 18.9 %collective-permute-start.16 = (bf16[80,4096]{1,0:T(8,128)(2,1)S(1)}, bf16[80,4096]{1,0:T(8,128)(2,1)S(1)}, u32[]{:S(2)}, u32[]{:S(2)}) collective-permute-start(bf16[80,4096]{1,0:T(8,128)(2,1)S(1)} %get-tuple-element.88), channel_id=1, source_target_pairs={{0,1},{1,32},{32,33},{33,0},{16,49},{17,16},{48,17},{49,48},{2,3},... | collective-permute-start | bytes 1966088 | tf_op jit(solution)/shard_map/ppermute | solution.py:32
  92.1 16.2 %collective-permute-start.19 = (bf16[64,4096]{1,0:T(8,128)(2,1)S(1)}, bf16[64,4096]{1,0:T(8,128)(2,1)S(1)}, u32[]{:S(2)}, u32[]{:S(2)}) collective-permute-start(bf16[64,4096]{1,0:T(8,128)(2,1)S(1)} %slice_select_fusion), channel_id=1, source_target_pairs={{0,2},{2,4},{4,6},{6,8},{8,10},{10,12},{12,14},{14,0},{16,30},{18,... | collective-permute-start | bytes 1572872 | tf_op jit(solution)/shard_map/ppermute | solution.py:354
  92.1 16.1 %collective-permute-start.17 = (bf16[48,4096]{1,0:T(8,128)(2,1)S(1)}, bf16[48,4096]{1,0:T(8,128)(2,1)S(1)}, u32[]{:S(2)}, u32[]{:S(2)}) collective-permute-start(bf16[48,4096]{1,0:T(8,128)(2,1)S(1)} %get-tuple-element.89), channel_id=1, source_target_pairs={{0,33},{1,0},{32,1},{33,32},{16,17},{17,48},{48,49},{49,16},{2,35}... | collective-permute-start | bytes 1179656 | tf_op jit(solution)/shard_map/ppermute | solution.py:32
  95.3 13.0 %collective-permute-start.18 = (bf16[16,4096]{1,0:T(8,128)(2,1)S(1)}, bf16[16,4096]{1,0:T(8,128)(2,1)S(1)}, u32[]{:S(2)}, u32[]{:S(2)}) collective-permute-start(bf16[16,4096]{1,0:T(8,128)(2,1)S(1)} %get-tuple-element.90), channel_id=1, source_target_pairs={{0,32},{1,33},{32,0},{33,1},{16,48},{17,49},{48,16},{49,17},{2,34}... | collective-permute-start | bytes 393224 | tf_op jit(solution)/shard_map/ppermute | solution.py:32
  126.7 13.9 %collective-permute-start.24 = (bf16[512,256]{1,0:T(8,128)(2,1)S(1)}, bf16[512,256]{1,0:T(8,128)(2,1)S(1)}, u32[]{:S(2)}, u32[]{:S(2)}) collective-permute-start(bf16[512,256]{1,0:T(8,128)(2,1)S(1)} %get-tuple-element.103), channel_id=1, source_target_pairs={{0,128},{64,192},{128,0},{192,64},{16,144},{80,208},{144,16},{208,... | collective-permute-start | bytes 786440 | tf_op jit(solution)/shard_map/ppermute | solution.py:25
  128.8 22.2 %collective-permute-start.28 = (bf16[512,256]{1,0:T(8,128)(2,1)S(1)}, bf16[512,256]{1,0:T(8,128)(2,1)S(1)}, u32[]{:S(2)}, u32[]{:S(2)}) collective-permute-start(bf16[512,256]{1,0:T(8,128)(2,1)S(1)} %get-tuple-element.107), channel_id=1, source_target_pairs={{0,128},{64,192},{128,0},{192,64},{16,144},{80,208},{144,16},{208,... | collective-permute-start | bytes 786440 | tf_op jit(solution)/shard_map/ppermute | solution.py:25
  130.4 15.0 %collective-permute-start.26 = (bf16[512,256]{1,0:T(8,128)(2,1)S(1)}, bf16[512,256]{1,0:T(8,128)(2,1)S(1)}, u32[]{:S(2)}, u32[]{:S(2)}) collective-permute-start(bf16[512,256]{1,0:T(8,128)(2,1)S(1)} %get-tuple-element.116), channel_id=1, source_target_pairs={{0,64},{64,128},{128,192},{192,0},{16,208},{80,16},{144,80},{208,1... | collective-permute-start | bytes 786440 | tf_op jit(solution)/shard_map/ppermute | solution.py:25
  145.5 10.7 %collective-permute-start.30 = (bf16[512,256]{1,0:T(8,128)(2,1)S(1)}, bf16[512,256]{1,0:T(8,128)(2,1)S(1)}, u32[]{:S(2)}, u32[]{:S(2)}) collective-permute-start(bf16[512,256]{1,0:T(8,128)(2,1)S(1)} %add_convert_fusion), channel_id=1, source_target_pairs={{0,32},{32,0},{1,33},{33,1},{2,34},{34,2},{3,35},{35,3},{4,36},{36... | collective-permute-start | bytes 786440 | tf_op jit(solution)/shard_map/ppermute | solution.py:40
  (27 other events, 240.5 us)
Sparse Core Ops, SparseCore 0:
  11.8 36.5 all-gather.4
  50.2 34.6 all-gather.6
where the time goes:
time: 168 us; the launch traced here: 166 us
  waiting for transfers between devices  72.2 us (43%)
  starting transfers between devices  39.9 us (24%)
  Pallas kernels  29.4 us (18%)
  between operations  13.8 us (8%)
  local copies, waits for them, and re-layouts  7.38 us (4%)
  other arithmetic  2.83 us (2%)
    ppermute x9, waiting for transfers between devices, along_y(): return lax.ppermute(v, ('yh', 'c', 'yl'), ring_perm(spots, step))  26.8 us
    ppermute x3, waiting for transfers between devices, swap_yh(): return lax.ppermute(v, 'yh', [(0, 1), (1, 0)])  19.5 us
    pallas_call x2, Pallas kernels, second_factor(): pl.pallas_call(lambda *refs: second_kernel(scale, layout, *refs), out_sha...  14.9 us
    ppermute x8, starting transfers between devices, shift_z(): return lax.ppermute(v, 'z', [(i, (i + step) % NZ) for i in range(NZ)])  14.6 us
    ppermute x6, waiting for transfers between devices, along_x(): lax.ppermute(v, ('x', 'c'), ring_perm([[x * 2 + c for x in range(NX)] for...  14.5 us
    ppermute x8, waiting for transfers between devices, shift_z(): return lax.ppermute(v, 'z', [(i, (i + step) % NZ) for i in range(NZ)])  11.4 us
    ppermute x9, starting transfers between devices, along_y(): return lax.ppermute(v, ('yh', 'c', 'yl'), ring_perm(spots, step))  10.3 us
    pallas_call x4, Pallas kernels, partials(): pl.pallas_call(lambda *refs: partial_kernel(len(EARLY), *refs), grid=(2,)...  9.95 us
  transfers between devices with their start and end apart: 33, of which 13 were waited for; matrix products, arithmetic and copies ran while one was open for 2% of the time, Pallas kernels for 12%

commit v1 on v0

--- a/solution.py
+++ b/solution.py
@@ -110,7 +110,8 @@
 def second_kernel(scale, layout, *refs):
     count = len(layout)
     arrays = refs[:count]
-    keep, recv, cot_keep, cot_recv, out, nsc, wsc, cabs, csc, nsem, wsem, csem = refs[count:]
+    keep, recv, cot_keep, cot_recv, out, laid = refs[count : count + 6]
+    nsc, wsc, cabs, csc, nsem, wsem, csem, osem = refs[count + 6 :]
     x, yh, c, z, yl = (lax.axis_index(a) for a in AXES)
     y = yh * 2 + yl
     group, units = cot_keep.shape
@@ -155,9 +156,12 @@
             place += 16
     for op in wait_w:
         op.wait()
+    wait_o = []
     for t in range(nsc.shape[0] // BLOCK):
         while wait_n and wait_n[0][0] < (t + 1) * BLOCK:
             wait_n.pop(0)[1].wait()
+        rows = pl.ds(t * BLOCK, BLOCK)
+        wait_o.append(copy(nsc.at[rows], laid.at[rows], osem.at[t]))
         block = nsc[t * BLOCK : (t + 1) * BLOCK, :]
 
         def mul(j):
@@ -174,6 +178,8 @@
             out[p * units : (p + 1) * units, t * BLOCK : (t + 1) * BLOCK] = second.T.astype(
                 jnp.bfloat16
             )
+    for op in wait_o:
+        op.wait()
 
 
 def second_factor(name, layout, arrays, keep, recv, cot_keep, cot_recv, scale):
@@ -183,9 +189,12 @@
     operands = (*arrays, keep, recv, cot_keep, cot_recv)
     return pl.pallas_call(
         lambda *refs: second_kernel(scale, layout, *refs),
-        out_shape=jax.ShapeDtypeStruct((2 * units, tokens), jnp.bfloat16),
+        out_shape=(
+            jax.ShapeDtypeStruct((2 * units, tokens), jnp.bfloat16),
+            jax.ShapeDtypeStruct((tokens, depth), jnp.bfloat16),
+        ),
         in_specs=[pl.BlockSpec(memory_space=pl.ANY)] * len(operands),
-        out_specs=pl.BlockSpec(memory_space=pltpu.VMEM),
+        out_specs=(pl.BlockSpec(memory_space=pltpu.VMEM), pl.BlockSpec(memory_space=pl.ANY)),
         scratch_shapes=[
             pltpu.VMEM((tokens, depth), jnp.bfloat16),
             pltpu.VMEM((depth, 4 * units), jnp.bfloat16),
@@ -194,8 +203,9 @@
             pltpu.SemaphoreType.DMA((len(layout),)),
             pltpu.SemaphoreType.DMA((16,)),
             pltpu.SemaphoreType.DMA((2,)),
+            pltpu.SemaphoreType.DMA((tokens // BLOCK,)),
         ],
-        compiler_params=pltpu.CompilerParams(vmem_limit_bytes=32 * 1024 * 1024),
+        compiler_params=pltpu.CompilerParams(vmem_limit_bytes=24 * 1024 * 1024),
         cost_estimate=pl.CostEstimate(
             flops=2**20, bytes_accessed=2**20, transcendentals=0
         ),
@@ -203,12 +213,9 @@
     )(*operands)
 
 
-def partial_kernel(early_count, *refs):
-    arrays, second_e, second_l, own, sib = refs[:-4], refs[-4], refs[-3], refs[-2], refs[-1]
-    early = jnp.concatenate([a[...] for a in arrays[:early_count]], axis=0)
-    late = jnp.concatenate([a[...] for a in arrays[early_count:]], axis=0)
-    result = jnp.dot(second_e[...], early, preferred_element_type=jnp.float32)
-    result = result + jnp.dot(second_l[...], late, preferred_element_type=jnp.float32)
+def partial_kernel(tokens_e, tokens_l, second_e, second_l, own, sib):
+    result = jnp.dot(second_e[...], tokens_e[...], preferred_element_type=jnp.float32)
+    result = result + jnp.dot(second_l[...], tokens_l[...], preferred_element_type=jnp.float32)
     result = result.astype(jnp.bfloat16)
     step = pl.program_id(0)
 
@@ -221,24 +228,23 @@
         sib[...] = result
 
 
-def partials(arrays, second_e, second_l, r):
+def partials(tokens_e, tokens_l, second_e, second_l, r):
     width = second_e.shape[0]
-    rows = rows_of(EARLY + LATE)
     half = jax.ShapeDtypeStruct((width, 512), jnp.bfloat16)
     whole = pl.BlockSpec((width, 512), lambda j: (0, 0))
     return pl.pallas_call(
-        lambda *refs: partial_kernel(len(EARLY), *refs),
+        partial_kernel,
         grid=(2,),
         out_shape=(half, half),
-        in_specs=[pl.BlockSpec((n, 512), lambda j: (0, r * 2 + j)) for n in rows]
+        in_specs=[
+            pl.BlockSpec((a.shape[0], 512), lambda j: (0, r * 2 + j)) for a in (tokens_e, tokens_l)
+        ]
         + [pl.BlockSpec(a.shape, lambda j: (0, 0)) for a in (second_e, second_l)],
         out_specs=(whole, whole),
-        compiler_params=pltpu.CompilerParams(vmem_limit_bytes=24 * 1024 * 1024),
-        cost_estimate=pl.CostEstimate(
-            flops=2**20, bytes_accessed=2**20, transcendentals=0
-        ),
+        compiler_params=pltpu.CompilerParams(vmem_limit_bytes=12 * 1024 * 1024),
+        cost_estimate=pl.CostEstimate(flops=2**20, bytes_accessed=2**20, transcendentals=0),
         name="partials_%d" % r,
-    )(*arrays, second_e, second_l)
+    )(tokens_e, tokens_l, second_e, second_l)
 
 
 def final_kernel(m0, m1, m2, m3, got, out):
@@ -295,7 +301,7 @@
             pl.BlockSpec((sum(pieces[i][2] for i in part), depth), lambda j: (0, 0))
             for part in parts
         ],
-        compiler_params=pltpu.CompilerParams(vmem_limit_bytes=24 * 1024 * 1024),
+        compiler_params=pltpu.CompilerParams(vmem_limit_bytes=12 * 1024 * 1024),
         name=name,
     )(*[a for a, _, _ in pieces])
 
@@ -321,8 +327,6 @@
     )
     p0, p1 = probes[:, 0, :], probes[:, 1, :]
     w_keep, w_send = half_of(yh), half_of(1 - yh)
-    cot_keep = lax.dynamic_slice_in_dim(cotangent, yh * units, units, 1)
-    cot_send = lax.dynamic_slice_in_dim(cotangent, (1 - yh) * units, units, 1)
     keep = lax.all_gather(w_keep, ("x", "c"))
 
     ya = [along_y(a0, i) for i in (1, 2, 3)]
@@ -337,10 +341,13 @@
     )
     up1, down1 = shift_z(up0, 1), shift_z(down0, -1)
     y1 = along_y(y0, 1)
-    up1, down1, y1, w_recv = ordered((up1, down1, y1, w_recv))
+    up1, down1, y1, w_recv, cotangent = ordered((up1, down1, y1, w_recv, cotangent))
     recv = lax.all_gather(w_recv, ("x", "c"))
 
     up2, down2 = shift_z(up1, 1), shift_z(down1, -1)
+    cot_keep = lax.dynamic_slice_in_dim(cotangent, yh * units, units, 1)
+    cot_send = lax.dynamic_slice_in_dim(cotangent, (1 - yh) * units, units, 1)
+    y1, cot_send = ordered((y1, cot_send))
     (y,) = lay("lay_2", [(y1, 0, 48), (up1, 64, 16), (down1, 64, 16)], ((0, 1, 2),))
     y2 = along_y(y, 1)
     up2, down2, y2, cot_send = ordered((up2, down2, y2, cot_send))
@@ -368,10 +375,9 @@
 
     scale = 1.0 / math.sqrt(cotangent.shape[0] * NX * NYH * NC)
     rest = (keep, recv, cot_keep, cot_recv, scale)
-    second_e = second_factor("second_early", EARLY, early, *rest)
-    second_l = second_factor("second_late", LATE, late, *rest)
+    second_e, tokens_e = second_factor("second_early", EARLY, early, *rest)
+    second_l, tokens_l = second_factor("second_late", LATE, late, *rest)
     own, sib, first, last = {}, {}, {}, {}
-    arrays = early + late
 
     def add_cores(r):
         other = swap_core(sib[(NX - r) % NX])
@@ -381,22 +387,21 @@
             pair = [v.astype(jnp.bfloat16) for v in pair]
         return ordered(pair[0]), ordered(pair[1])
 
-    own[2], sib[2] = partials(arrays, second_e, second_l, 2)
-    own[3], sib[3] = partials(arrays, second_e, second_l, 3)
+    for r in (2, 3):
+        own[r], sib[r] = partials(tokens_e, tokens_l, second_e, second_l, r)
     first[2], last[2] = add_cores(2)
     first[2], last[2], second_l = ordered((first[2], last[2], second_l))
-    own[1], sib[1] = partials(arrays, second_e, second_l, 1)
-    first[1], last[1] = add_cores(1)
-    first[1], second_l = ordered((first[1], second_l))
-    own[0], sib[0] = partials(arrays, second_e, second_l, 0)
-    first[3], last[3] = add_cores(3)
-    first[0], last[0] = add_cores(0)
-    last[2] = along_x(last[2], NX - 2)
-    for r in (2, 1, 3):
-        first[r] = along_x(first[r], NX - r)
-    *arrived, last[1], last[3] = ordered((*(first[r] for r in range(NX)), last[1], last[3]))
+    for r in (1, 0):
+        own[r], sib[r] = partials(tokens_e, tokens_l, second_e, second_l, r)
+    for r in (2, 3, 1, 0):
+        if r != 2:
+            first[r], last[r] = add_cores(r)
+        if r:
+            first[r] = along_x(first[r], NX - r)
+    last[1] = along_x(last[1], NX - 1)
+    *arrived, last[2], last[3] = ordered((*(first[r] for r in range(NX)), last[2], last[3]))
     total = sum(v.astype(jnp.float32) for v in arrived)
-    for r in (1, 3):
+    for r in (2, 3):
         last[r] = along_x(last[r], NX - r)
     got = swap_yh(total.astype(jnp.bfloat16))
     return finish([last[r] for r in range(NX)], got)

time: 168 us -> 161 us (0.958)
  waiting for transfers between devices: 72.2 us -> 62.6 us
  starting transfers between devices: 39.9 us -> 45.1 us
  Pallas kernels: 29.4 us -> 27 us
    ppermute x9, waiting for transfers between devices: 26.8 us -> 16.6 us  [along_y(): return lax.ppermute(v, ('yh', 'c', 'yl'), ring_perm(spots, step))]
    ppermute x3, waiting for transfers between devices: 19.5 us -> 14.7 us  [swap_yh(): return lax.ppermute(v, 'yh', [(0, 1), (1, 0)])]
    pallas_call x4, Pallas kernels: 9.95 us -> 6.88 us  [partials(): pl.pallas_call(partial_kernel, grid=(2,), out_shape=(half, half), in_spec...]
    ppermute x8, waiting for transfers between devices: 11.4 us -> 14.3 us  [shift_z(): return lax.ppermute(v, 'z', [(i, (i + step) % NZ) for i in range(NZ)])]
    ppermute x6, waiting for transfers between devices: 14.5 us -> 16.9 us  [along_x(): lax.ppermute(v, ('x', 'c'), ring_perm([[x * 2 + c for x in range(NX)] for...]
    ppermute x3, starting transfers between devices: 4.64 us -> 6.98 us  [swap_yh(): return lax.ppermute(v, 'yh', [(0, 1), (1, 0)])]
  transfers between devices with their start and end apart: 33 -> 33, of which waited for: 13 -> 10; matrix products, arithmetic and copies ran while one was open for 2% -> 3% of each run, Pallas kernels for 12% -> 11%
where the time goes in v1:
time: 161 us; the launch traced here: 159 us
  waiting for transfers between devices  62.6 us (39%)
  starting transfers between devices  45.1 us (28%)
  Pallas kernels  27 us (17%)
  between operations  13.9 us (9%)
  local copies, waits for them, and re-layouts  7.56 us (5%)
  other arithmetic  2.83 us (2%)
    ppermute x6, waiting for transfers between devices, along_x(): lax.ppermute(v, ('x', 'c'), ring_perm([[x * 2 + c for x in range(NX)] for...  16.9 us
    ppermute x9, waiting for transfers between devices, along_y(): return lax.ppermute(v, ('yh', 'c', 'yl'), ring_perm(spots, step))  16.6 us
    ppermute x8, starting transfers between devices, shift_z(): return lax.ppermute(v, 'z', [(i, (i + step) % NZ) for i in range(NZ)])  15.7 us
    pallas_call x2, Pallas kernels, second_factor(): pl.pallas_call(lambda *refs: second_kernel(scale, layout, *refs), out_sha...  15.6 us
    ppermute x3, waiting for transfers between devices, swap_yh(): return lax.ppermute(v, 'yh', [(0, 1), (1, 0)])  14.7 us
    ppermute x8, waiting for transfers between devices, shift_z(): return lax.ppermute(v, 'z', [(i, (i + step) % NZ) for i in range(NZ)])  14.3 us
    ppermute x9, starting transfers between devices, along_y(): return lax.ppermute(v, ('yh', 'c', 'yl'), ring_perm(spots, step))  11.2 us
    ppermute x6, starting transfers between devices, along_x(): lax.ppermute(v, ('x', 'c'), ring_perm([[x * 2 + c for x in range(NX)] for...  8.48 us
  transfers between devices with their start and end apart: 33, of which 10 were waited for; matrix products, arithmetic and copies ran while one was open for 3% of the time, Pallas kernels for 11%

profile of v1, /device:TPU:2, one launch (start us, length us, event | category | flops | bytes accessed | tf_op | source)
XLA Modules:
  0.0 159.0 jit_solution(16017242157713114745)
XLA Ops:
  6.5 1.8 %rms_norm.1 = (bf16[16,4096]{1,0:T(8,128)(2,1)}, bf16[16,4096]{1,0:T(8,128)(2,1)}) custom-call(bf16[32,4096]{1,0:T(8,128)(2,1)} %tokens.1, f32[1,4096]{1,0:T(1,128)} %bitcast.15), custom_call_target="tpu_custom_call" | custom-call | tf_op jit(solution)/shard_map/rms_norm/pallas_call | solution.py:65
  13.4 2.9 %collective-permute-start.1 = (bf16[16,4096]{1,0:T(8,128)(2,1)S(1)}, bf16[16,4096]{1,0:T(8,128)(2,1)S(1)}, u32[]{:S(2)}, u32[]{:S(2)}) collective-permute-start(bf16[16,4096]{1,0:T(8,128)(2,1)S(1)} %copy-done.18), channel_id=1, source_target_pairs={{0,32},{1,33},{32,0},{33,1},{16,48},{17,49},{48,16},{49,17},{2,34}... | collective-permute-start | bytes 393224 | tf_op jit(solution)/shard_map/ppermute | solution.py:32
  17.6 1.9 %collective-permute-start.3 = (bf16[16,4096]{1,0:T(8,128)(2,1)S(1)}, bf16[16,4096]{1,0:T(8,128)(2,1)S(1)}, u32[]{:S(2)}, u32[]{:S(2)}) collective-permute-start(bf16[16,4096]{1,0:T(8,128)(2,1)S(1)} %copy-done.12), channel_id=1, source_target_pairs={{0,2},{2,4},{4,6},{6,8},{8,10},{10,12},{12,14},{14,0},{1,3},{3,5},... | collective-permute-start | bytes 393224 | tf_op jit(solution)/shard_map/ppermute | solution.py:310
  19.5 3.9 %collective-permute-start.4 = (bf16[16,4096]{1,0:T(8,128)(2,1)S(1)}, bf16[16,4096]{1,0:T(8,128)(2,1)S(1)}, u32[]{:S(2)}, u32[]{:S(2)}) collective-permute-start(bf16[16,4096]{1,0:T(8,128)(2,1)S(1)} %copy-done.12), channel_id=1, source_target_pairs={{0,14},{2,0},{4,2},{6,4},{8,6},{10,8},{12,10},{14,12},{1,15},{3,1}... | collective-permute-start | bytes 393224 | tf_op jit(solution)/shard_map/ppermute | solution.py:310
  23.6 2.8 %collective-permute-done.3.refs_4_.refs_8_ = bf16[16,4096]{1,0:T(8,128)(2,1)S(1)} collective-permute-done((bf16[16,4096]{1,0:T(8,128)(2,1)S(1)}, bf16[16,4096]{1,0:T(8,128)(2,1)S(1)}, u32[]{:S(2)}, u32[]{:S(2)}) %collective-permute-start.3) | collective-permute-done | bytes 131104 | tf_op jit(solution)/shard_map/ppermute | solution.py:310
  27.5 3.2 %collective-permute-start.6 = (bf16[80,4096]{1,0:T(8,128)(2,1)S(1)}, bf16[80,4096]{1,0:T(8,128)(2,1)S(1)}, u32[]{:S(2)}, u32[]{:S(2)}) collective-permute-start(bf16[80,4096]{1,0:T(8,128)(2,1)S(1)} %get-tuple-element.78), channel_id=1, source_target_pairs={{0,14},{2,0},{4,2},{6,4},{8,6},{10,8},{12,10},{14,12},{1,15},{3,1}... | collective-permute-start | bytes 1966088 | tf_op jit(solution)/shard_map/ppermute | solution.py:310
  32.3 16.5 %collective-permute-done.7.refs_0_ = bf16[48,4096]{1,0:T(8,128)(2,1)S(1)} collective-permute-done((bf16[48,4096]{1,0:T(8,128)(2,1)S(1)}, bf16[48,4096]{1,0:T(8,128)(2,1)S(1)}, u32[]{:S(2)}, u32[]{:S(2)}) %collective-permute-start.7) | collective-permute-done | bytes 393248 | tf_op jit(solution)/shard_map/ppermute | solution.py:32
  48.9 3.2 %collective-permute-start.10 = (bf16[80,4096]{1,0:T(8,128)(2,1)S(1)}, bf16[80,4096]{1,0:T(8,128)(2,1)S(1)}, u32[]{:S(2)}, u32[]{:S(2)}) collective-permute-start(bf16[80,4096]{1,0:T(8,128)(2,1)S(1)} %collective-permute-done.6.refs_2_), channel_id=1, source_target_pairs={{0,14},{2,0},{4,2},{6,4},{8,6},{10,8},{12,10},{14,12},{1,15},{3,1}... | collective-permute-start | bytes 1966088 | tf_op jit(solution)/shard_map/ppermute | solution.py:310
  52.2 1.9 %constant_dynamic-slice_fusion.2 = (bf16[512,256]{1,0:T(8,128)(2,1)}, bf16[512,256]{1,0:T(8,128)(2,1)}) fusion(bf16[512,512]{1,0:T(8,128)(2,1)} %param.11, s32[]{:T(128)S(6)} %select_n.11, s32[]{:T(128)S(6)} %select_n.10), kind=kLoop, calls=%fused_computation.20 | loop fusion | bytes 1048584 | tf_op jit(solution)/shard_map/dynamic_slice | solution.py:348
  54.4 11.4 %collective-permute-done.9.refs_1_.refs_3_.refs_5_ = bf16[80,4096]{1,0:T(8,128)(2,1)S(1)} collective-permute-done((bf16[80,4096]{1,0:T(8,128)(2,1)S(1)}, bf16[80,4096]{1,0:T(8,128)(2,1)S(1)}, u32[]{:S(2)}, u32[]{:S(2)}) %collective-permute-start.9) | collective-permute-done | bytes 655392 | tf_op jit(solution)/shard_map/ppermute | solution.py:310
  68.9 2.2 %collective-permute-start.13 = (bf16[80,4096]{1,0:T(8,128)(2,1)S(1)}, bf16[80,4096]{1,0:T(8,128)(2,1)}, u32[]{:S(2)}, u32[]{:S(2)}) collective-permute-start(bf16[80,4096]{1,0:T(8,128)(2,1)S(1)} %collective-permute-done.10.refs_2_.refs_4_.refs_6_), channel_id=1, source_target_pairs={{0,14},{2,0},{4,2},{6,4},{8,6},{10,8},{12,10},{14,12},{1,15},{3,1}... | collective-permute-start | bytes 1966088 | tf_op jit(solution)/shard_map/ppermute | solution.py:310
  71.1 2.8 %collective-permute-start.15 = (bf16[512,256]{1,0:T(8,128)(2,1)}, bf16[512,256]{1,0:T(8,128)(2,1)}, u32[]{:S(2)}, u32[]{:S(2)}) collective-permute-start(bf16[512,256]{1,0:T(8,128)(2,1)} %get-tuple-element.91), channel_id=1, source_target_pairs={{0,32},{32,0},{1,33},{33,1},{2,34},{34,2},{3,35},{35,3},{4,36},{36... | collective-permute-start | bytes 786440 | tf_op jit(solution)/shard_map/ppermute | solution.py:40
  73.9 14.1 %collective-permute-done.15.refs_15_.refs_8_ = bf16[512,256]{1,0:T(8,128)(2,1)} collective-permute-done((bf16[512,256]{1,0:T(8,128)(2,1)}, bf16[512,256]{1,0:T(8,128)(2,1)}, u32[]{:S(2)}, u32[]{:S(2)}) %collective-permute-start.15) | collective-permute-done | bytes 262176 | tf_op jit(solution)/shard_map/ppermute | solution.py:40
  90.7 3.1 %collective-permute-start.17 = (bf16[48,4096]{1,0:T(8,128)(2,1)S(1)}, bf16[48,4096]{1,0:T(8,128)(2,1)S(1)}, u32[]{:S(2)}, u32[]{:S(2)}) collective-permute-start(bf16[48,4096]{1,0:T(8,128)(2,1)S(1)} %get-tuple-element.101), channel_id=1, source_target_pairs={{0,33},{1,0},{32,1},{33,32},{16,17},{17,48},{48,49},{49,16},{2,35}... | collective-permute-start | bytes 1179656 | tf_op jit(solution)/shard_map/ppermute | solution.py:32
  93.8 2.2 %copy-done.1 = bf16[2048,1024]{1,0:T(8,128)(2,1)S(1)} copy-done((bf16[2048,1024]{1,0:T(8,128)(2,1)S(1)}, bf16[2048,1024]{1,0:T(8,128)(2,1)}, u32[]{:S(2)}) %copy-start.1) | copy-done | bytes 4194328
  96.0 11.2 %second_early.1 = (bf16[512,768]{1,0:T(8,128)(2,1)S(1)}, bf16[768,4096]{1,0:T(8,128)(2,1)S(1)}) custom-call(bf16[80,4096]{1,0:T(8,128)(2,1)S(1)} %copy-done.11, bf16[80,4096]{1,0:T(8,128)(2,1)S(1)} %collective-permute-done.5.refs_1_, bf16[80,4096]{1,0:T(8,128)(2,1)S(1)} %copy-done.4, bf16[80,4096]{1,0:T(8,128)(2,1)S(1)} %collective-permute-done.9.refs_1_.refs_3_.refs_5_, ...), custom_call_target="tpu_custom_call" | custom-call | flops 1048576 | bytes 1048576 | tf_op jit(solution)/shard_map/second_early/pallas_call | solution.py:190
  107.2 4.4 %second_late.1 = (bf16[512,256]{1,0:T(8,128)(2,1)S(1)}, bf16[256,4096]{1,0:T(8,128)(2,1)S(1)}) custom-call(bf16[48,4096]{1,0:T(8,128)(2,1)S(1)} %copy-done.9, bf16[80,4096]{1,0:T(8,128)(2,1)S(1)} %collective-permute-done.16.refs_1_, bf16[48,4096]{1,0:T(8,128)(2,1)S(1)} %collective-permute-done.17.refs_2_, ...), custom_call_target="tpu_custom_call" | custom-call | flops 1048576 | bytes 1048576 | tf_op jit(solution)/shard_map/second_late/pallas_call | solution.py:190
  122.1 2.0 %collective-permute-start.24 = (bf16[512,256]{1,0:T(8,128)(2,1)S(1)}, bf16[512,256]{1,0:T(8,128)(2,1)S(1)}, u32[]{:S(2)}, u32[]{:S(2)}) collective-permute-start(bf16[512,256]{1,0:T(8,128)(2,1)S(1)} %get-tuple-element.127), channel_id=1, source_target_pairs={{0,192},{64,0},{128,64},{192,128},{16,80},{80,144},{144,208},{208,... | collective-permute-start | bytes 786440 | tf_op jit(solution)/shard_map/ppermute | solution.py:25
  124.3 2.2 %collective-permute-start.27 = (bf16[512,256]{1,0:T(8,128)(2,1)S(1)}, bf16[512,256]{1,0:T(8,128)(2,1)S(1)}, u32[]{:S(2)}, u32[]{:S(2)}) collective-permute-start(bf16[512,256]{1,0:T(8,128)(2,1)S(1)} %get-tuple-element.126), channel_id=1, source_target_pairs={{0,64},{64,128},{128,192},{192,0},{16,208},{80,16},{144,80},{208,1... | collective-permute-start | bytes 786440 | tf_op jit(solution)/shard_map/ppermute | solution.py:25
  126.8 9.3 %collective-permute-done.24 = bf16[512,256]{1,0:T(8,128)(2,1)S(1)} collective-permute-done((bf16[512,256]{1,0:T(8,128)(2,1)S(1)}, bf16[512,256]{1,0:T(8,128)(2,1)S(1)}, u32[]{:S(2)}, u32[]{:S(2)}) %collective-permute-start.24) | collective-permute-done | bytes 262176 | tf_op jit(solution)/shard_map/ppermute | solution.py:25
  136.1 3.1 %collective-permute-done.25 = bf16[512,256]{1,0:T(8,128)(2,1)S(1)} collective-permute-done((bf16[512,256]{1,0:T(8,128)(2,1)S(1)}, bf16[512,256]{1,0:T(8,128)(2,1)S(1)}, u32[]{:S(2)}, u32[]{:S(2)}) %collective-permute-start.25) | collective-permute-done | bytes 262176 | tf_op jit(solution)/shard_map/ppermute | solution.py:25
  139.2 2.6 %collective-permute-start.28 = (bf16[512,256]{1,0:T(8,128)(2,1)S(1)}, bf16[512,256]{1,0:T(8,128)(2,1)S(1)}, u32[]{:S(2)}, u32[]{:S(2)}) collective-permute-start(bf16[512,256]{1,0:T(8,128)(2,1)S(1)} %get-tuple-element.117), channel_id=1, source_target_pairs={{0,128},{64,192},{128,0},{192,64},{16,144},{80,208},{144,16},{208,... | collective-permute-start | bytes 786440 | tf_op jit(solution)/shard_map/ppermute | solution.py:25
  142.0 3.5 %collective-permute-start.30 = (bf16[512,256]{1,0:T(8,128)(2,1)S(1)}, bf16[512,256]{1,0:T(8,128)(2,1)S(1)}, u32[]{:S(2)}, u32[]{:S(2)}) collective-permute-start(bf16[512,256]{1,0:T(8,128)(2,1)S(1)} %add_convert_fusion), channel_id=1, source_target_pairs={{0,32},{32,0},{1,33},{33,1},{2,34},{34,2},{3,35},{35,3},{4,36},{36... | collective-permute-start | bytes 786440 | tf_op jit(solution)/shard_map/ppermute | solution.py:40
  145.5 3.7 %collective-permute-done.28.m2 = bf16[512,256]{1,0:T(8,128)(2,1)S(1)} collective-permute-done((bf16[512,256]{1,0:T(8,128)(2,1)S(1)}, bf16[512,256]{1,0:T(8,128)(2,1)S(1)}, u32[]{:S(2)}, u32[]{:S(2)}) %collective-permute-start.28) | collective-permute-done | bytes 262176 | tf_op jit(solution)/shard_map/ppermute | solution.py:25
  (111 shorter events, 29.2 us)
Async XLA Ops:
  6.5 81.5 %all-gather.5.cloned.1.call-start = ((), (), s32[]{:S(2)}) async-start(), calls=%async_computation | async-start | bytes 4718592 | tf_op jit(solution)/shard_map/all_gather | solution.py:330
  11.6 76.4 %all-gather.7.cloned.1.call-start = ((), (), s32[]{:S(2)}) async-start(), calls=%async_computation.1 | async-start | bytes 4718592 | tf_op jit(solution)/shard_map/all_gather | solution.py:345
  11.7 11.8 %collective-permute-start = (bf16[16,4096]{1,0:T(8,128)(2,1)S(1)}, bf16[16,4096]{1,0:T(8,128)(2,1)S(1)}, u32[]{:S(2)}, u32[]{:S(2)}) collective-permute-start(bf16[16,4096]{1,0:T(8,128)(2,1)S(1)} %copy-done.18), channel_id=1, source_target_pairs={{0,1},{1,32},{32,33},{33,0},{16,49},{17,16},{48,17},{49,48},{2,3},... | collective-permute-start | bytes 393224 | tf_op jit(solution)/shard_map/ppermute | solution.py:32
  13.4 10.2 %collective-permute-start.1 = (bf16[16,4096]{1,0:T(8,128)(2,1)S(1)}, bf16[16,4096]{1,0:T(8,128)(2,1)S(1)}, u32[]{:S(2)}, u32[]{:S(2)}) collective-permute-start(bf16[16,4096]{1,0:T(8,128)(2,1)S(1)} %copy-done.18), channel_id=1, source_target_pairs={{0,32},{1,33},{32,0},{33,1},{16,48},{17,49},{48,16},{49,17},{2,34}... | collective-permute-start | bytes 393224 | tf_op jit(solution)/shard_map/ppermute | solution.py:32
  26.5 22.3 %collective-permute-start.5 = (bf16[80,4096]{1,0:T(8,128)(2,1)S(1)}, bf16[80,4096]{1,0:T(8,128)(2,1)S(1)}, u32[]{:S(2)}, u32[]{:S(2)}) collective-permute-start(bf16[80,4096]{1,0:T(8,128)(2,1)S(1)} %get-tuple-element.77.refs_0_), channel_id=1, source_target_pairs={{0,2},{2,4},{4,6},{6,8},{8,10},{10,12},{12,14},{14,0},{1,3},{3,5},... | collective-permute-start | bytes 1966088 | tf_op jit(solution)/shard_map/ppermute | solution.py:310
  27.5 21.3 %collective-permute-start.6 = (bf16[80,4096]{1,0:T(8,128)(2,1)S(1)}, bf16[80,4096]{1,0:T(8,128)(2,1)S(1)}, u32[]{:S(2)}, u32[]{:S(2)}) collective-permute-start(bf16[80,4096]{1,0:T(8,128)(2,1)S(1)} %get-tuple-element.78), channel_id=1, source_target_pairs={{0,14},{2,0},{4,2},{6,4},{8,6},{10,8},{12,10},{14,12},{1,15},{3,1}... | collective-permute-start | bytes 1966088 | tf_op jit(solution)/shard_map/ppermute | solution.py:310
  30.7 18.1 %collective-permute-start.8 = (bf16[256,1024]{1,0:T(8,128)(2,1)S(1)}, bf16[256,1024]{1,0:T(8,128)(2,1)}, u32[]{:S(2)}, u32[]{:S(2)}) collective-permute-start(bf16[256,1024]{1,0:T(8,128)(2,1)S(1)} %pad_maximum_fusion), channel_id=1, source_target_pairs={{0,32},{32,0},{1,33},{33,1},{2,34},{34,2},{3,35},{35,3},{4,36},{36... | collective-permute-start | bytes 1572872 | tf_op jit(solution)/shard_map/ppermute | solution.py:40
  31.4 17.4 %collective-permute-start.7 = (bf16[48,4096]{1,0:T(8,128)(2,1)S(1)}, bf16[48,4096]{1,0:T(8,128)(2,1)S(1)}, u32[]{:S(2)}, u32[]{:S(2)}) collective-permute-start(bf16[48,4096]{1,0:T(8,128)(2,1)S(1)} %get-tuple-element.79), channel_id=1, source_target_pairs={{0,1},{1,32},{32,33},{33,0},{16,49},{17,16},{48,17},{49,48},{2,3},... | collective-permute-start | bytes 1179656 | tf_op jit(solution)/shard_map/ppermute | solution.py:32
  48.8 17.0 %collective-permute-start.9 = (bf16[80,4096]{1,0:T(8,128)(2,1)S(1)}, bf16[80,4096]{1,0:T(8,128)(2,1)S(1)}, u32[]{:S(2)}, u32[]{:S(2)}) collective-permute-start(bf16[80,4096]{1,0:T(8,128)(2,1)S(1)} %collective-permute-done.5.refs_1_), channel_id=1, source_target_pairs={{0,2},{2,4},{4,6},{6,8},{8,10},{10,12},{12,14},{14,0},{1,3},{3,5},... | collective-permute-start | bytes 1966088 | tf_op jit(solution)/shard_map/ppermute | solution.py:310
  48.9 16.9 %collective-permute-start.10 = (bf16[80,4096]{1,0:T(8,128)(2,1)S(1)}, bf16[80,4096]{1,0:T(8,128)(2,1)S(1)}, u32[]{:S(2)}, u32[]{:S(2)}) collective-permute-start(bf16[80,4096]{1,0:T(8,128)(2,1)S(1)} %collective-permute-done.6.refs_2_), channel_id=1, source_target_pairs={{0,14},{2,0},{4,2},{6,4},{8,6},{10,8},{12,10},{14,12},{1,15},{3,1}... | collective-permute-start | bytes 1966088 | tf_op jit(solution)/shard_map/ppermute | solution.py:310
  54.1 11.9 %collective-permute-start.11 = (bf16[80,4096]{1,0:T(8,128)(2,1)S(1)}, bf16[80,4096]{1,0:T(8,128)(2,1)S(1)}, u32[]{:S(2)}, u32[]{:S(2)}) collective-permute-start(bf16[80,4096]{1,0:T(8,128)(2,1)S(1)} %lay_2.1), channel_id=1, source_target_pairs={{0,1},{1,32},{32,33},{33,0},{16,49},{17,16},{48,17},{49,48},{2,3},... | collective-permute-start | bytes 1966088 | tf_op jit(solution)/shard_map/ppermute | solution.py:32
  67.0 21.0 %collective-permute-start.14 = (bf16[112,4096]{1,0:T(8,128)(2,1)}, bf16[112,4096]{1,0:T(8,128)(2,1)S(1)}, u32[]{:S(2)}, u32[]{:S(2)}) collective-permute-start(bf16[112,4096]{1,0:T(8,128)(2,1)} %lay_3.1), channel_id=1, source_target_pairs={{0,1},{1,32},{32,33},{33,0},{16,49},{17,16},{48,17},{49,48},{2,3},... | collective-permute-start | bytes 2752520 | tf_op jit(solution)/shard_map/ppermute | solution.py:32
  67.9 20.1 %collective-permute-start.12 = (bf16[80,4096]{1,0:T(8,128)(2,1)S(1)}, bf16[80,4096]{1,0:T(8,128)(2,1)S(1)}, u32[]{:S(2)}, u32[]{:S(2)}) collective-permute-start(bf16[80,4096]{1,0:T(8,128)(2,1)S(1)} %collective-permute-done.9.refs_1_.refs_3_.refs_5_), channel_id=1, source_target_pairs={{0,2},{2,4},{4,6},{6,8},{8,10},{10,12},{12,14},{14,0},{1,3},{3,5},... | collective-permute-start | bytes 1966088 | tf_op jit(solution)/shard_map/ppermute | solution.py:310
  68.9 19.1 %collective-permute-start.13 = (bf16[80,4096]{1,0:T(8,128)(2,1)S(1)}, bf16[80,4096]{1,0:T(8,128)(2,1)}, u32[]{:S(2)}, u32[]{:S(2)}) collective-permute-start(bf16[80,4096]{1,0:T(8,128)(2,1)S(1)} %collective-permute-done.10.refs_2_.refs_4_.refs_6_), channel_id=1, source_target_pairs={{0,14},{2,0},{4,2},{6,4},{8,6},{10,8},{12,10},{14,12},{1,15},{3,1}... | collective-permute-start | bytes 1966088 | tf_op jit(solution)/shard_map/ppermute | solution.py:310
  71.1 16.9 %collective-permute-start.15 = (bf16[512,256]{1,0:T(8,128)(2,1)}, bf16[512,256]{1,0:T(8,128)(2,1)}, u32[]{:S(2)}, u32[]{:S(2)}) collective-permute-start(bf16[512,256]{1,0:T(8,128)(2,1)} %get-tuple-element.91), channel_id=1, source_target_pairs={{0,32},{32,0},{1,33},{33,1},{2,34},{34,2},{3,35},{35,3},{4,36},{36... | collective-permute-start | bytes 786440 | tf_op jit(solution)/shard_map/ppermute | solution.py:40
  88.2 19.0 %collective-permute-start.16 = (bf16[80,4096]{1,0:T(8,128)(2,1)S(1)}, bf16[80,4096]{1,0:T(8,128)(2,1)S(1)}, u32[]{:S(2)}, u32[]{:S(2)}) collective-permute-start(bf16[80,4096]{1,0:T(8,128)(2,1)S(1)} %get-tuple-element.100), channel_id=1, source_target_pairs={{0,1},{1,32},{32,33},{33,0},{16,49},{17,16},{48,17},{49,48},{2,3},... | collective-permute-start | bytes 1966088 | tf_op jit(solution)/shard_map/ppermute | solution.py:32
  89.6 17.6 %collective-permute-start.19 = (bf16[64,4096]{1,0:T(8,128)(2,1)S(1)}, bf16[64,4096]{1,0:T(8,128)(2,1)S(1)}, u32[]{:S(2)}, u32[]{:S(2)}) collective-permute-start(bf16[64,4096]{1,0:T(8,128)(2,1)S(1)} %slice_select_fusion), channel_id=1, source_target_pairs={{0,2},{2,4},{4,6},{6,8},{8,10},{10,12},{12,14},{14,0},{16,30},{18,... | collective-permute-start | bytes 1572872 | tf_op jit(solution)/shard_map/ppermute | solution.py:361
  90.7 16.5 %collective-permute-start.17 = (bf16[48,4096]{1,0:T(8,128)(2,1)S(1)}, bf16[48,4096]{1,0:T(8,128)(2,1)S(1)}, u32[]{:S(2)}, u32[]{:S(2)}) collective-permute-start(bf16[48,4096]{1,0:T(8,128)(2,1)S(1)} %get-tuple-element.101), channel_id=1, source_target_pairs={{0,33},{1,0},{32,1},{33,32},{16,17},{17,48},{48,49},{49,16},{2,35}... | collective-permute-start | bytes 1179656 | tf_op jit(solution)/shard_map/ppermute | solution.py:32
  93.7 13.4 %collective-permute-start.18 = (bf16[16,4096]{1,0:T(8,128)(2,1)S(1)}, bf16[16,4096]{1,0:T(8,128)(2,1)S(1)}, u32[]{:S(2)}, u32[]{:S(2)}) collective-permute-start(bf16[16,4096]{1,0:T(8,128)(2,1)S(1)} %get-tuple-element.102), channel_id=1, source_target_pairs={{0,32},{1,33},{32,0},{33,1},{16,48},{17,49},{48,16},{49,17},{2,34}... | collective-permute-start | bytes 393224 | tf_op jit(solution)/shard_map/ppermute | solution.py:32
  120.5 24.9 %collective-permute-start.23 = (bf16[512,256]{1,0:T(8,128)(2,1)S(1)}, bf16[512,256]{1,0:T(8,128)(2,1)S(1)}, u32[]{:S(2)}, u32[]{:S(2)}) collective-permute-start(bf16[512,256]{1,0:T(8,128)(2,1)S(1)} %get-tuple-element.128), channel_id=1, source_target_pairs={{0,192},{64,0},{128,64},{192,128},{16,80},{80,144},{144,208},{208,... | collective-permute-start | bytes 786440 | tf_op jit(solution)/shard_map/ppermute | solution.py:25
  122.1 14.0 %collective-permute-start.24 = (bf16[512,256]{1,0:T(8,128)(2,1)S(1)}, bf16[512,256]{1,0:T(8,128)(2,1)S(1)}, u32[]{:S(2)}, u32[]{:S(2)}) collective-permute-start(bf16[512,256]{1,0:T(8,128)(2,1)S(1)} %get-tuple-element.127), channel_id=1, source_target_pairs={{0,192},{64,0},{128,64},{192,128},{16,80},{80,144},{144,208},{208,... | collective-permute-start | bytes 786440 | tf_op jit(solution)/shard_map/ppermute | solution.py:25
  124.1 15.0 %collective-permute-start.25 = (bf16[512,256]{1,0:T(8,128)(2,1)S(1)}, bf16[512,256]{1,0:T(8,128)(2,1)S(1)}, u32[]{:S(2)}, u32[]{:S(2)}) collective-permute-start(bf16[512,256]{1,0:T(8,128)(2,1)S(1)} %get-tuple-element.113), channel_id=1, source_target_pairs={{0,128},{64,192},{128,0},{192,64},{16,144},{80,208},{144,16},{208,... | collective-permute-start | bytes 786440 | tf_op jit(solution)/shard_map/ppermute | solution.py:25
  124.3 14.8 %collective-permute-start.27 = (bf16[512,256]{1,0:T(8,128)(2,1)S(1)}, bf16[512,256]{1,0:T(8,128)(2,1)S(1)}, u32[]{:S(2)}, u32[]{:S(2)}) collective-permute-start(bf16[512,256]{1,0:T(8,128)(2,1)S(1)} %get-tuple-element.126), channel_id=1, source_target_pairs={{0,64},{64,128},{128,192},{192,0},{16,208},{80,16},{144,80},{208,1... | collective-permute-start | bytes 786440 | tf_op jit(solution)/shard_map/ppermute | solution.py:25
  139.2 10.0 %collective-permute-start.28 = (bf16[512,256]{1,0:T(8,128)(2,1)S(1)}, bf16[512,256]{1,0:T(8,128)(2,1)S(1)}, u32[]{:S(2)}, u32[]{:S(2)}) collective-permute-start(bf16[512,256]{1,0:T(8,128)(2,1)S(1)} %get-tuple-element.117), channel_id=1, source_target_pairs={{0,128},{64,192},{128,0},{192,64},{16,144},{80,208},{144,16},{208,... | collective-permute-start | bytes 786440 | tf_op jit(solution)/shard_map/ppermute | solution.py:25
  (28 other events, 190.3 us)
Sparse Core Ops, SparseCore 0:
  11.8 36.5 all-gather.4
  50.2 34.6 all-gather.6

commit v2 on v1

--- a/solution.py
+++ b/solution.py
@@ -353,13 +353,17 @@
     up2, down2, y2, cot_send = ordered((up2, down2, y2, cot_send))
     cot_recv = swap_yh(cot_send)
 
-    up3, down3 = shift_z(up2, 1), shift_z(down2, -1)
-    (y,) = lay("lay_3", [(y2, 0, 80), (up2, 64, 16), (down2, 64, 16)], ((0, 1, 2),))
+    y, down = lay(
+        "lay_3",
+        [(y2, 0, 80), (up2, 64, 16), (down2, 64, 16), (down2, 0, 64)],
+        ((0, 1, 2), (3,)),
+    )
+    up3, down3 = shift_z(up2, 1), shift_z(down, -1)
     y3 = along_y(y, 1)
     up3, down3, y3, cot_recv, keep, recv = ordered((up3, down3, y3, cot_recv, keep, recv))
 
     a4 = lax.ppermute(
-        jnp.where(c == 0, up3[:64], down3[:64]),
+        jnp.where(c == 0, up3[:64], down3),
         ("c", "z"),
         ring_perm([[i * NZ + z for z in range(NZ)] for i in range(NC)], 1),
     )

time: 161 us -> 160 us (level)
  waiting for transfers between devices: 62.6 us -> 65.8 us
  starting transfers between devices: 45.1 us -> 42.8 us
    ppermute x6, waiting for transfers between devices: 16.9 us -> 19 us  [along_x(): lax.ppermute(v, ('x', 'c'), ring_perm([[x * 2 + c for x in range(NX)] for...]
    ppermute x3, starting transfers between devices: 6.98 us -> 5.08 us  [swap_yh(): return lax.ppermute(v, 'yh', [(0, 1), (1, 0)])]
  transfers between devices with their start and end apart: 33 -> 33, of which waited for: 10 -> 11; matrix products, arithmetic and copies ran while one was open for 3% -> 2% of each run, Pallas kernels for 11% -> 11%
where the time goes in v2:
time: 160 us; the launch traced here: 159 us
  waiting for transfers between devices  65.8 us (41%)
  starting transfers between devices  42.8 us (27%)
  Pallas kernels  27.3 us (17%)
  between operations  13.8 us (9%)
  local copies, waits for them, and re-layouts  7.54 us (5%)
  other arithmetic  1.63 us (1%)
    ppermute x6, waiting for transfers between devices, along_x(): lax.ppermute(v, ('x', 'c'), ring_perm([[x * 2 + c for x in range(NX)] for...  19 us
    ppermute x9, waiting for transfers between devices, along_y(): return lax.ppermute(v, ('yh', 'c', 'yl'), ring_perm(spots, step))  18 us
    ppermute x8, starting transfers between devices, shift_z(): return lax.ppermute(v, 'z', [(i, (i + step) % NZ) for i in range(NZ)])  15.7 us
    pallas_call x2, Pallas kernels, second_factor(): pl.pallas_call(lambda *refs: second_kernel(scale, layout, *refs), out_sha...  15.5 us
    ppermute x3, waiting for transfers between devices, swap_yh(): return lax.ppermute(v, 'yh', [(0, 1), (1, 0)])  14.4 us
    ppermute x8, waiting for transfers between devices, shift_z(): return lax.ppermute(v, 'z', [(i, (i + step) % NZ) for i in range(NZ)])  14.3 us
    ppermute x9, starting transfers between devices, along_y(): return lax.ppermute(v, ('yh', 'c', 'yl'), ring_perm(spots, step))  11.8 us
    ppermute x6, starting transfers between devices, along_x(): lax.ppermute(v, ('x', 'c'), ring_perm([[x * 2 + c for x in range(NX)] for...  8.37 us
  transfers between devices with their start and end apart: 33, of which 11 were waited for; matrix products, arithmetic and copies ran while one was open for 2% of the time, Pallas kernels for 11%

profile of v2, /device:TPU:2, one launch (start us, length us, event | category | flops | bytes accessed | tf_op | source)
XLA Modules:
  0.0 158.8 jit_solution(6436082247952541210)
XLA Ops:
  6.5 1.8 %rms_norm.1 = (bf16[16,4096]{1,0:T(8,128)(2,1)}, bf16[16,4096]{1,0:T(8,128)(2,1)}) custom-call(bf16[32,4096]{1,0:T(8,128)(2,1)} %tokens.1, f32[1,4096]{1,0:T(1,128)} %bitcast.15), custom_call_target="tpu_custom_call" | custom-call | tf_op jit(solution)/shard_map/rms_norm/pallas_call | solution.py:65
  13.3 2.9 %collective-permute-start.1 = (bf16[16,4096]{1,0:T(8,128)(2,1)S(1)}, bf16[16,4096]{1,0:T(8,128)(2,1)S(1)}, u32[]{:S(2)}, u32[]{:S(2)}) collective-permute-start(bf16[16,4096]{1,0:T(8,128)(2,1)S(1)} %copy-done.18), channel_id=1, source_target_pairs={{0,32},{1,33},{32,0},{33,1},{16,48},{17,49},{48,16},{49,17},{2,34}... | collective-permute-start | bytes 393224 | tf_op jit(solution)/shard_map/ppermute | solution.py:32
  17.6 1.9 %collective-permute-start.3 = (bf16[16,4096]{1,0:T(8,128)(2,1)S(1)}, bf16[16,4096]{1,0:T(8,128)(2,1)S(1)}, u32[]{:S(2)}, u32[]{:S(2)}) collective-permute-start(bf16[16,4096]{1,0:T(8,128)(2,1)S(1)} %copy-done.12), channel_id=1, source_target_pairs={{0,2},{2,4},{4,6},{6,8},{8,10},{10,12},{12,14},{14,0},{1,3},{3,5},... | collective-permute-start | bytes 393224 | tf_op jit(solution)/shard_map/ppermute | solution.py:310
  19.5 3.9 %collective-permute-start.4 = (bf16[16,4096]{1,0:T(8,128)(2,1)S(1)}, bf16[16,4096]{1,0:T(8,128)(2,1)S(1)}, u32[]{:S(2)}, u32[]{:S(2)}) collective-permute-start(bf16[16,4096]{1,0:T(8,128)(2,1)S(1)} %copy-done.12), channel_id=1, source_target_pairs={{0,14},{2,0},{4,2},{6,4},{8,6},{10,8},{12,10},{14,12},{1,15},{3,1}... | collective-permute-start | bytes 393224 | tf_op jit(solution)/shard_map/ppermute | solution.py:310
  23.5 2.8 %collective-permute-done.3.refs_4_.refs_8_ = bf16[16,4096]{1,0:T(8,128)(2,1)S(1)} collective-permute-done((bf16[16,4096]{1,0:T(8,128)(2,1)S(1)}, bf16[16,4096]{1,0:T(8,128)(2,1)S(1)}, u32[]{:S(2)}, u32[]{:S(2)}) %collective-permute-start.3) | collective-permute-done | bytes 131104 | tf_op jit(solution)/shard_map/ppermute | solution.py:310
  27.5 3.2 %collective-permute-start.6 = (bf16[80,4096]{1,0:T(8,128)(2,1)S(1)}, bf16[80,4096]{1,0:T(8,128)(2,1)S(1)}, u32[]{:S(2)}, u32[]{:S(2)}) collective-permute-start(bf16[80,4096]{1,0:T(8,128)(2,1)S(1)} %get-tuple-element.80), channel_id=1, source_target_pairs={{0,14},{2,0},{4,2},{6,4},{8,6},{10,8},{12,10},{14,12},{1,15},{3,1}... | collective-permute-start | bytes 1966088 | tf_op jit(solution)/shard_map/ppermute | solution.py:310
  32.3 16.5 %collective-permute-done.7.refs_0_ = bf16[48,4096]{1,0:T(8,128)(2,1)S(1)} collective-permute-done((bf16[48,4096]{1,0:T(8,128)(2,1)S(1)}, bf16[48,4096]{1,0:T(8,128)(2,1)S(1)}, u32[]{:S(2)}, u32[]{:S(2)}) %collective-permute-start.7) | collective-permute-done | bytes 393248 | tf_op jit(solution)/shard_map/ppermute | solution.py:32
  48.9 3.2 %collective-permute-start.10 = (bf16[80,4096]{1,0:T(8,128)(2,1)S(1)}, bf16[80,4096]{1,0:T(8,128)(2,1)S(1)}, u32[]{:S(2)}, u32[]{:S(2)}) collective-permute-start(bf16[80,4096]{1,0:T(8,128)(2,1)S(1)} %collective-permute-done.6.refs_2_), channel_id=1, source_target_pairs={{0,14},{2,0},{4,2},{6,4},{8,6},{10,8},{12,10},{14,12},{1,15},{3,1}... | collective-permute-start | bytes 1966088 | tf_op jit(solution)/shard_map/ppermute | solution.py:310
  52.1 1.8 %constant_dynamic-slice_fusion.2 = (bf16[512,256]{1,0:T(8,128)(2,1)}, bf16[512,256]{1,0:T(8,128)(2,1)}) fusion(bf16[512,512]{1,0:T(8,128)(2,1)} %param.11, s32[]{:T(128)S(6)} %select_n.11, s32[]{:T(128)S(6)} %select_n.10), kind=kLoop, calls=%fused_computation.20 | loop fusion | bytes 1048584 | tf_op jit(solution)/shard_map/dynamic_slice | solution.py:348
  54.3 11.5 %collective-permute-done.9.refs_1_.refs_3_.refs_5_ = bf16[80,4096]{1,0:T(8,128)(2,1)S(1)} collective-permute-done((bf16[80,4096]{1,0:T(8,128)(2,1)S(1)}, bf16[80,4096]{1,0:T(8,128)(2,1)S(1)}, u32[]{:S(2)}, u32[]{:S(2)}) %collective-permute-start.9) | collective-permute-done | bytes 655392 | tf_op jit(solution)/shard_map/ppermute | solution.py:310
  69.2 2.2 %collective-permute-start.13 = (bf16[64,4096]{1,0:T(8,128)(2,1)}, bf16[64,4096]{1,0:T(8,128)(2,1)}, u32[]{:S(2)}, u32[]{:S(2)}) collective-permute-start(bf16[64,4096]{1,0:T(8,128)(2,1)} %get-tuple-element.93), channel_id=1, source_target_pairs={{0,14},{2,0},{4,2},{6,4},{8,6},{10,8},{12,10},{14,12},{1,15},{3,1}... | collective-permute-start | bytes 1572872 | tf_op jit(solution)/shard_map/ppermute | solution.py:310
  71.3 2.8 %collective-permute-start.15 = (bf16[512,256]{1,0:T(8,128)(2,1)}, bf16[512,256]{1,0:T(8,128)(2,1)}, u32[]{:S(2)}, u32[]{:S(2)}) collective-permute-start(bf16[512,256]{1,0:T(8,128)(2,1)} %get-tuple-element.95), channel_id=1, source_target_pairs={{0,32},{32,0},{1,33},{33,1},{2,34},{34,2},{3,35},{35,3},{4,36},{36... | collective-permute-start | bytes 786440 | tf_op jit(solution)/shard_map/ppermute | solution.py:40
  74.2 14.1 %collective-permute-done.15.refs_15_.refs_8_ = bf16[512,256]{1,0:T(8,128)(2,1)} collective-permute-done((bf16[512,256]{1,0:T(8,128)(2,1)}, bf16[512,256]{1,0:T(8,128)(2,1)}, u32[]{:S(2)}, u32[]{:S(2)}) %collective-permute-start.15) | collective-permute-done | bytes 262176 | tf_op jit(solution)/shard_map/ppermute | solution.py:40
  88.7 3.3 %collective-permute-start.17 = (bf16[48,4096]{1,0:T(8,128)(2,1)S(1)}, bf16[48,4096]{1,0:T(8,128)(2,1)S(1)}, u32[]{:S(2)}, u32[]{:S(2)}) collective-permute-start(bf16[48,4096]{1,0:T(8,128)(2,1)S(1)} %get-tuple-element.105), channel_id=1, source_target_pairs={{0,33},{1,0},{32,1},{33,32},{16,17},{17,48},{48,49},{49,16},{2,35}... | collective-permute-start | bytes 1179656 | tf_op jit(solution)/shard_map/ppermute | solution.py:32
  92.5 2.2 %copy-done.1 = bf16[2048,1024]{1,0:T(8,128)(2,1)S(1)} copy-done((bf16[2048,1024]{1,0:T(8,128)(2,1)S(1)}, bf16[2048,1024]{1,0:T(8,128)(2,1)}, u32[]{:S(2)}) %copy-start.1) | copy-done | bytes 4194328
  94.7 11.2 %second_early.1 = (bf16[512,768]{1,0:T(8,128)(2,1)S(1)}, bf16[768,4096]{1,0:T(8,128)(2,1)S(1)}) custom-call(bf16[80,4096]{1,0:T(8,128)(2,1)S(1)} %copy-done.11, bf16[80,4096]{1,0:T(8,128)(2,1)S(1)} %collective-permute-done.5.refs_1_, bf16[80,4096]{1,0:T(8,128)(2,1)S(1)} %copy-done.4, bf16[80,4096]{1,0:T(8,128)(2,1)S(1)} %collective-permute-done.9.refs_1_.refs_3_.refs_5_, ...), custom_call_target="tpu_custom_call" | custom-call | flops 1048576 | bytes 1048576 | tf_op jit(solution)/shard_map/second_early/pallas_call | solution.py:190
  107.3 4.4 %second_late.1 = (bf16[512,256]{1,0:T(8,128)(2,1)S(1)}, bf16[256,4096]{1,0:T(8,128)(2,1)S(1)}) custom-call(bf16[48,4096]{1,0:T(8,128)(2,1)S(1)} %copy-done.9, bf16[80,4096]{1,0:T(8,128)(2,1)S(1)} %collective-permute-done.16.refs_1_, bf16[48,4096]{1,0:T(8,128)(2,1)S(1)} %collective-permute-done.17.refs_2_, ...), custom_call_target="tpu_custom_call" | custom-call | flops 1048576 | bytes 1048576 | tf_op jit(solution)/shard_map/second_late/pallas_call | solution.py:190
  111.7 1.7 %partials_2.1 = (bf16[512,512]{1,0:T(8,128)(2,1)S(1)}, bf16[512,512]{1,0:T(8,128)(2,1)S(1)}) custom-call(bf16[768,4096]{1,0:T(8,128)(2,1)S(1)} %get-tuple-element.103.tokens_e, bf16[256,4096]{1,0:T(8,128)(2,1)S(1)} %get-tuple-element.107.tokens_l, bf16[512,768]{1,0:T(8,128)(2,1)S(1)} %get-tuple-element.108.second_e, ...), custom_call_target="tpu_custom_call" | custom-call | flops 1048576 | bytes 1048576 | tf_op jit(solution)/shard_map/partials_2/pallas_call | solution.py:235
  122.1 1.9 %collective-permute-start.24 = (bf16[512,256]{1,0:T(8,128)(2,1)S(1)}, bf16[512,256]{1,0:T(8,128)(2,1)S(1)}, u32[]{:S(2)}, u32[]{:S(2)}) collective-permute-start(bf16[512,256]{1,0:T(8,128)(2,1)S(1)} %get-tuple-element.131), channel_id=1, source_target_pairs={{0,192},{64,0},{128,64},{192,128},{16,80},{80,144},{144,208},{208,... | collective-permute-start | bytes 786440 | tf_op jit(solution)/shard_map/ppermute | solution.py:25
  124.4 2.2 %collective-permute-start.27 = (bf16[512,256]{1,0:T(8,128)(2,1)S(1)}, bf16[512,256]{1,0:T(8,128)(2,1)S(1)}, u32[]{:S(2)}, u32[]{:S(2)}) collective-permute-start(bf16[512,256]{1,0:T(8,128)(2,1)S(1)} %get-tuple-element.130), channel_id=1, source_target_pairs={{0,64},{64,128},{128,192},{192,0},{16,208},{80,16},{144,80},{208,1... | collective-permute-start | bytes 786440 | tf_op jit(solution)/shard_map/ppermute | solution.py:25
  126.8 9.7 %collective-permute-done.24 = bf16[512,256]{1,0:T(8,128)(2,1)S(1)} collective-permute-done((bf16[512,256]{1,0:T(8,128)(2,1)S(1)}, bf16[512,256]{1,0:T(8,128)(2,1)S(1)}, u32[]{:S(2)}, u32[]{:S(2)}) %collective-permute-start.24) | collective-permute-done | bytes 262176 | tf_op jit(solution)/shard_map/ppermute | solution.py:25
  136.5 2.8 %collective-permute-done.25 = bf16[512,256]{1,0:T(8,128)(2,1)S(1)} collective-permute-done((bf16[512,256]{1,0:T(8,128)(2,1)S(1)}, bf16[512,256]{1,0:T(8,128)(2,1)S(1)}, u32[]{:S(2)}, u32[]{:S(2)}) %collective-permute-start.25) | collective-permute-done | bytes 262176 | tf_op jit(solution)/shard_map/ppermute | solution.py:25
  139.3 2.4 %collective-permute-start.28 = (bf16[512,256]{1,0:T(8,128)(2,1)S(1)}, bf16[512,256]{1,0:T(8,128)(2,1)S(1)}, u32[]{:S(2)}, u32[]{:S(2)}) collective-permute-start(bf16[512,256]{1,0:T(8,128)(2,1)S(1)} %get-tuple-element.121), channel_id=1, source_target_pairs={{0,128},{64,192},{128,0},{192,64},{16,144},{80,208},{144,16},{208,... | collective-permute-start | bytes 786440 | tf_op jit(solution)/shard_map/ppermute | solution.py:25
  143.6 5.7 %collective-permute-done.28.m2 = bf16[512,256]{1,0:T(8,128)(2,1)S(1)} collective-permute-done((bf16[512,256]{1,0:T(8,128)(2,1)S(1)}, bf16[512,256]{1,0:T(8,128)(2,1)S(1)}, u32[]{:S(2)}, u32[]{:S(2)}) %collective-permute-start.28) | collective-permute-done | bytes 262176 | tf_op jit(solution)/shard_map/ppermute | solution.py:25
  (111 shorter events, 29.0 us)
Async XLA Ops:
  6.5 81.7 %all-gather.5.cloned.1.call-start = ((), (), s32[]{:S(2)}) async-start(), calls=%async_computation | async-start | bytes 4718592 | tf_op jit(solution)/shard_map/all_gather | solution.py:330
  11.6 76.6 %all-gather.7.cloned.1.call-start = ((), (), s32[]{:S(2)}) async-start(), calls=%async_computation.1 | async-start | bytes 4718592 | tf_op jit(solution)/shard_map/all_gather | solution.py:345
  11.7 11.8 %collective-permute-start = (bf16[16,4096]{1,0:T(8,128)(2,1)S(1)}, bf16[16,4096]{1,0:T(8,128)(2,1)S(1)}, u32[]{:S(2)}, u32[]{:S(2)}) collective-permute-start(bf16[16,4096]{1,0:T(8,128)(2,1)S(1)} %copy-done.18), channel_id=1, source_target_pairs={{0,1},{1,32},{32,33},{33,0},{16,49},{17,16},{48,17},{49,48},{2,3},... | collective-permute-start | bytes 393224 | tf_op jit(solution)/shard_map/ppermute | solution.py:32
  13.3 10.2 %collective-permute-start.1 = (bf16[16,4096]{1,0:T(8,128)(2,1)S(1)}, bf16[16,4096]{1,0:T(8,128)(2,1)S(1)}, u32[]{:S(2)}, u32[]{:S(2)}) collective-permute-start(bf16[16,4096]{1,0:T(8,128)(2,1)S(1)} %copy-done.18), channel_id=1, source_target_pairs={{0,32},{1,33},{32,0},{33,1},{16,48},{17,49},{48,16},{49,17},{2,34}... | collective-permute-start | bytes 393224 | tf_op jit(solution)/shard_map/ppermute | solution.py:32
  26.5 22.3 %collective-permute-start.5 = (bf16[80,4096]{1,0:T(8,128)(2,1)S(1)}, bf16[80,4096]{1,0:T(8,128)(2,1)S(1)}, u32[]{:S(2)}, u32[]{:S(2)}) collective-permute-start(bf16[80,4096]{1,0:T(8,128)(2,1)S(1)} %get-tuple-element.79.refs_0_), channel_id=1, source_target_pairs={{0,2},{2,4},{4,6},{6,8},{8,10},{10,12},{12,14},{14,0},{1,3},{3,5},... | collective-permute-start | bytes 1966088 | tf_op jit(solution)/shard_map/ppermute | solution.py:310
  27.5 21.3 %collective-permute-start.6 = (bf16[80,4096]{1,0:T(8,128)(2,1)S(1)}, bf16[80,4096]{1,0:T(8,128)(2,1)S(1)}, u32[]{:S(2)}, u32[]{:S(2)}) collective-permute-start(bf16[80,4096]{1,0:T(8,128)(2,1)S(1)} %get-tuple-element.80), channel_id=1, source_target_pairs={{0,14},{2,0},{4,2},{6,4},{8,6},{10,8},{12,10},{14,12},{1,15},{3,1}... | collective-permute-start | bytes 1966088 | tf_op jit(solution)/shard_map/ppermute | solution.py:310
  30.7 18.1 %collective-permute-start.8 = (bf16[256,1024]{1,0:T(8,128)(2,1)S(1)}, bf16[256,1024]{1,0:T(8,128)(2,1)}, u32[]{:S(2)}, u32[]{:S(2)}) collective-permute-start(bf16[256,1024]{1,0:T(8,128)(2,1)S(1)} %pad_maximum_fusion), channel_id=1, source_target_pairs={{0,32},{32,0},{1,33},{33,1},{2,34},{34,2},{3,35},{35,3},{4,36},{36... | collective-permute-start | bytes 1572872 | tf_op jit(solution)/shard_map/ppermute | solution.py:40
  31.4 17.4 %collective-permute-start.7 = (bf16[48,4096]{1,0:T(8,128)(2,1)S(1)}, bf16[48,4096]{1,0:T(8,128)(2,1)S(1)}, u32[]{:S(2)}, u32[]{:S(2)}) collective-permute-start(bf16[48,4096]{1,0:T(8,128)(2,1)S(1)} %get-tuple-element.81), channel_id=1, source_target_pairs={{0,1},{1,32},{32,33},{33,0},{16,49},{17,16},{48,17},{49,48},{2,3},... | collective-permute-start | bytes 1179656 | tf_op jit(solution)/shard_map/ppermute | solution.py:32
  48.8 17.0 %collective-permute-start.9 = (bf16[80,4096]{1,0:T(8,128)(2,1)S(1)}, bf16[80,4096]{1,0:T(8,128)(2,1)S(1)}, u32[]{:S(2)}, u32[]{:S(2)}) collective-permute-start(bf16[80,4096]{1,0:T(8,128)(2,1)S(1)} %collective-permute-done.5.refs_1_), channel_id=1, source_target_pairs={{0,2},{2,4},{4,6},{6,8},{8,10},{10,12},{12,14},{14,0},{1,3},{3,5},... | collective-permute-start | bytes 1966088 | tf_op jit(solution)/shard_map/ppermute | solution.py:310
  48.9 16.9 %collective-permute-start.10 = (bf16[80,4096]{1,0:T(8,128)(2,1)S(1)}, bf16[80,4096]{1,0:T(8,128)(2,1)S(1)}, u32[]{:S(2)}, u32[]{:S(2)}) collective-permute-start(bf16[80,4096]{1,0:T(8,128)(2,1)S(1)} %collective-permute-done.6.refs_2_), channel_id=1, source_target_pairs={{0,14},{2,0},{4,2},{6,4},{8,6},{10,8},{12,10},{14,12},{1,15},{3,1}... | collective-permute-start | bytes 1966088 | tf_op jit(solution)/shard_map/ppermute | solution.py:310
  54.0 11.9 %collective-permute-start.11 = (bf16[80,4096]{1,0:T(8,128)(2,1)S(1)}, bf16[80,4096]{1,0:T(8,128)(2,1)S(1)}, u32[]{:S(2)}, u32[]{:S(2)}) collective-permute-start(bf16[80,4096]{1,0:T(8,128)(2,1)S(1)} %lay_2.1), channel_id=1, source_target_pairs={{0,1},{1,32},{32,33},{33,0},{16,49},{17,16},{48,17},{49,48},{2,3},... | collective-permute-start | bytes 1966088 | tf_op jit(solution)/shard_map/ppermute | solution.py:32
  67.2 21.0 %collective-permute-start.14 = (bf16[112,4096]{1,0:T(8,128)(2,1)}, bf16[112,4096]{1,0:T(8,128)(2,1)S(1)}, u32[]{:S(2)}, u32[]{:S(2)}) collective-permute-start(bf16[112,4096]{1,0:T(8,128)(2,1)} %get-tuple-element.94), channel_id=1, source_target_pairs={{0,1},{1,32},{32,33},{33,0},{16,49},{17,16},{48,17},{49,48},{2,3},... | collective-permute-start | bytes 2752520 | tf_op jit(solution)/shard_map/ppermute | solution.py:32
  68.1 20.1 %collective-permute-start.12 = (bf16[80,4096]{1,0:T(8,128)(2,1)S(1)}, bf16[80,4096]{1,0:T(8,128)(2,1)S(1)}, u32[]{:S(2)}, u32[]{:S(2)}) collective-permute-start(bf16[80,4096]{1,0:T(8,128)(2,1)S(1)} %collective-permute-done.9.refs_1_.refs_3_.refs_5_), channel_id=1, source_target_pairs={{0,2},{2,4},{4,6},{6,8},{8,10},{10,12},{12,14},{14,0},{1,3},{3,5},... | collective-permute-start | bytes 1966088 | tf_op jit(solution)/shard_map/ppermute | solution.py:310
  69.2 19.1 %collective-permute-start.13 = (bf16[64,4096]{1,0:T(8,128)(2,1)}, bf16[64,4096]{1,0:T(8,128)(2,1)}, u32[]{:S(2)}, u32[]{:S(2)}) collective-permute-start(bf16[64,4096]{1,0:T(8,128)(2,1)} %get-tuple-element.93), channel_id=1, source_target_pairs={{0,14},{2,0},{4,2},{6,4},{8,6},{10,8},{12,10},{14,12},{1,15},{3,1}... | collective-permute-start | bytes 1572872 | tf_op jit(solution)/shard_map/ppermute | solution.py:310
  71.3 16.9 %collective-permute-start.15 = (bf16[512,256]{1,0:T(8,128)(2,1)}, bf16[512,256]{1,0:T(8,128)(2,1)}, u32[]{:S(2)}, u32[]{:S(2)}) collective-permute-start(bf16[512,256]{1,0:T(8,128)(2,1)} %get-tuple-element.95), channel_id=1, source_target_pairs={{0,32},{32,0},{1,33},{33,1},{2,34},{34,2},{3,35},{35,3},{4,36},{36... | collective-permute-start | bytes 786440 | tf_op jit(solution)/shard_map/ppermute | solution.py:40
  88.4 18.9 %collective-permute-start.16 = (bf16[80,4096]{1,0:T(8,128)(2,1)S(1)}, bf16[80,4096]{1,0:T(8,128)(2,1)S(1)}, u32[]{:S(2)}, u32[]{:S(2)}) collective-permute-start(bf16[80,4096]{1,0:T(8,128)(2,1)S(1)} %get-tuple-element.104), channel_id=1, source_target_pairs={{0,1},{1,32},{32,33},{33,0},{16,49},{17,16},{48,17},{49,48},{2,3},... | collective-permute-start | bytes 1966088 | tf_op jit(solution)/shard_map/ppermute | solution.py:32
  88.6 17.3 %collective-permute-start.19 = (bf16[64,4096]{1,0:T(8,128)(2,1)S(1)}, bf16[64,4096]{1,0:T(8,128)(2,1)S(1)}, u32[]{:S(2)}, u32[]{:S(2)}) collective-permute-start(bf16[64,4096]{1,0:T(8,128)(2,1)S(1)} %slice_select_fusion), channel_id=1, source_target_pairs={{0,2},{2,4},{4,6},{6,8},{8,10},{10,12},{12,14},{14,0},{16,30},{18,... | collective-permute-start | bytes 1572872 | tf_op jit(solution)/shard_map/ppermute | solution.py:365
  88.7 17.2 %collective-permute-start.17 = (bf16[48,4096]{1,0:T(8,128)(2,1)S(1)}, bf16[48,4096]{1,0:T(8,128)(2,1)S(1)}, u32[]{:S(2)}, u32[]{:S(2)}) collective-permute-start(bf16[48,4096]{1,0:T(8,128)(2,1)S(1)} %get-tuple-element.105), channel_id=1, source_target_pairs={{0,33},{1,0},{32,1},{33,32},{16,17},{17,48},{48,49},{49,16},{2,35}... | collective-permute-start | bytes 1179656 | tf_op jit(solution)/shard_map/ppermute | solution.py:32
  92.0 13.9 %collective-permute-start.18 = (bf16[16,4096]{1,0:T(8,128)(2,1)S(1)}, bf16[16,4096]{1,0:T(8,128)(2,1)S(1)}, u32[]{:S(2)}, u32[]{:S(2)}) collective-permute-start(bf16[16,4096]{1,0:T(8,128)(2,1)S(1)} %get-tuple-element.106), channel_id=1, source_target_pairs={{0,32},{1,33},{32,0},{33,1},{16,48},{17,49},{48,16},{49,17},{2,34}... | collective-permute-start | bytes 393224 | tf_op jit(solution)/shard_map/ppermute | solution.py:32
  120.6 22.9 %collective-permute-start.23 = (bf16[512,256]{1,0:T(8,128)(2,1)S(1)}, bf16[512,256]{1,0:T(8,128)(2,1)S(1)}, u32[]{:S(2)}, u32[]{:S(2)}) collective-permute-start(bf16[512,256]{1,0:T(8,128)(2,1)S(1)} %get-tuple-element.132), channel_id=1, source_target_pairs={{0,192},{64,0},{128,64},{192,128},{16,80},{80,144},{144,208},{208,... | collective-permute-start | bytes 786440 | tf_op jit(solution)/shard_map/ppermute | solution.py:25
  122.1 14.4 %collective-permute-start.24 = (bf16[512,256]{1,0:T(8,128)(2,1)S(1)}, bf16[512,256]{1,0:T(8,128)(2,1)S(1)}, u32[]{:S(2)}, u32[]{:S(2)}) collective-permute-start(bf16[512,256]{1,0:T(8,128)(2,1)S(1)} %get-tuple-element.131), channel_id=1, source_target_pairs={{0,192},{64,0},{128,64},{192,128},{16,80},{80,144},{144,208},{208,... | collective-permute-start | bytes 786440 | tf_op jit(solution)/shard_map/ppermute | solution.py:25
  124.0 15.2 %collective-permute-start.25 = (bf16[512,256]{1,0:T(8,128)(2,1)S(1)}, bf16[512,256]{1,0:T(8,128)(2,1)S(1)}, u32[]{:S(2)}, u32[]{:S(2)}) collective-permute-start(bf16[512,256]{1,0:T(8,128)(2,1)S(1)} %get-tuple-element.117), channel_id=1, source_target_pairs={{0,128},{64,192},{128,0},{192,64},{16,144},{80,208},{144,16},{208,... | collective-permute-start | bytes 786440 | tf_op jit(solution)/shard_map/ppermute | solution.py:25
  124.4 14.9 %collective-permute-start.27 = (bf16[512,256]{1,0:T(8,128)(2,1)S(1)}, bf16[512,256]{1,0:T(8,128)(2,1)S(1)}, u32[]{:S(2)}, u32[]{:S(2)}) collective-permute-start(bf16[512,256]{1,0:T(8,128)(2,1)S(1)} %get-tuple-element.130), channel_id=1, source_target_pairs={{0,64},{64,128},{128,192},{192,0},{16,208},{80,16},{144,80},{208,1... | collective-permute-start | bytes 786440 | tf_op jit(solution)/shard_map/ppermute | solution.py:25
  139.3 10.0 %collective-permute-start.28 = (bf16[512,256]{1,0:T(8,128)(2,1)S(1)}, bf16[512,256]{1,0:T(8,128)(2,1)S(1)}, u32[]{:S(2)}, u32[]{:S(2)}) collective-permute-start(bf16[512,256]{1,0:T(8,128)(2,1)S(1)} %get-tuple-element.121), channel_id=1, source_target_pairs={{0,128},{64,192},{128,0},{192,64},{16,144},{80,208},{144,16},{208,... | collective-permute-start | bytes 786440 | tf_op jit(solution)/shard_map/ppermute | solution.py:25
  (28 other events, 183.7 us)
Sparse Core Ops, SparseCore 0:
  11.7 36.5 all-gather.4
  50.2 34.6 all-gather.6
